TPU v7x, 512 devices: a whole 4x8x8 slice. The times are simulated.
512 devices in a mesh: dp: 8 (over y), expert: 64 (over x, z, core).
Axes of the slice: x: 4, y: 8, z: 8, core: 2. Of those that a mesh axis runs over, the one named last changes fastest.
Arguments:
- tokens: bfloat16 [65536, 4096], P(('dp', 'expert'))
- routes: int32 [65536, 8], P(('dp', 'expert')), may hold values from 0 to 127, as said below
- old_slots: int32 [64], replicated, may hold values from 0 to 63, each once
- new_slots: int32 [64], replicated, may hold values from 0 to 63, each once
- weights: bfloat16 [64, 1536, 4096], P('expert', None, 'dp'), may hold values from -6 to 6
- patterns: int32 [64, 1536, 32], P('expert'), may hold values from 0 to 5
- inverse: float32 [64, 128, 128], P('expert'), as said below
Outputs:
- new_weights: bfloat16 [64, 1536, 4096], P('expert', None, 'dp')
Inputs may be any that keep to these rules, and one draw needn't show every extreme that they name: `routes`: each row names 8 distinct experts; within the 128 rows of one device no expert is named by more than 9 rows, and some expert below 64 is named by exactly 9 rows of every device. `old_slots`: each of 0 to 63 once. `new_slots`: each of 0 to 63 once. `inverse`: symmetric.
All inputs are finite; a program needn't handle non-finite values.
Results may differ from a plain program's by a relative error of at most 0.001.
Values may be sent and summed in bfloat16 or wider, within the bound.
No kernel may reach another device: no remote copies, remote signals or barrier semaphores. Data moves between devices by JAX's collectives and lax.ppermute only.
A program may use at most 64 MiB of HBM per device.

v0:
```python
import jax
import jax.numpy as jnp
import numpy as np
from jax import lax
from jax.sharding import PartitionSpec as P

D = 4096
PANEL = 128
CAP = 9


KEEP_PAIRS = np.array(
    [[1, 1, 0, 0], [1, 0, 1, 0], [1, 0, 0, 1], [0, 1, 1, 0], [0, 1, 0, 1], [0, 0, 1, 1]]
)
EPSILON = 1e-06
DAMPING = 0.01


def spread_2(value, axis, root):
    mine = lax.axis_index(axis) == root
    return lax.psum(jnp.where(mine, value, jnp.zeros_like(value)), axis)


def mask_from(pattern):
    onehot = (pattern[..., None] == jnp.arange(6, dtype=jnp.int32)).astype(jnp.float32)
    table = jnp.asarray(KEEP_PAIRS, dtype=jnp.float32)
    picked = jnp.sum(onehot[..., :, None] * table, axis=-2)
    return picked.reshape(pattern.shape[0], -1)


def slot_rows(block_routes, wanted, capacity):
    count_rows = block_routes.shape[0]
    matched = jnp.any(block_routes[:, :, None] == wanted[None, None, :], axis=1).astype(jnp.int32)
    ranked = jnp.cumsum(matched, axis=0, dtype=jnp.int32) - 1
    places = jnp.arange(capacity, dtype=jnp.int32)
    chosen = (matched.T[:, None, :] == 1) & (ranked.T[:, None, :] == places[None, :, None])
    row_ids = jnp.arange(count_rows, dtype=jnp.int32)
    indices = jnp.sum(jnp.where(chosen, row_ids[None, None, :], 0), axis=-1)
    filled = jnp.any(chosen, axis=-1)
    return (indices, filled)


def panel_solve(panel_held, mask, gram_panel, inverse_block):
    panel_part = panel_held.astype(jnp.float32)
    dropped = (1.0 - mask) * panel_part
    damped = gram_panel + DAMPING * jnp.eye(PANEL, dtype=jnp.float32)
    step_one = jnp.dot(dropped, damped, precision=lax.Precision.HIGHEST)
    refitted = mask * (
        panel_part + jnp.dot(step_one, inverse_block, precision=lax.Precision.HIGHEST)
    )
    return (refitted, refitted - panel_part)


def row_products(left, right):
    return lax.dot_general(
        left, right, (((0,), (0,)), ((), ())), preferred_element_type=jnp.float32
    )


def shards(tokens, routes, old_slots, new_slots, weights, patterns, inverse):
    owners = lax.axis_size("expert")
    group_index = lax.axis_index("dp")
    held = weights[0]
    columns = held.shape[1]
    indices, filled = slot_rows(routes, old_slots, CAP)
    outgoing = jnp.where(filled[..., None], jnp.take(tokens, indices, axis=0), 0)
    arrived = lax.all_to_all(outgoing, "expert", split_axis=0, concat_axis=0, tiled=True)
    gathered = arrived.reshape(-1, tokens.shape[1])
    gram_part = row_products(gathered, gathered[:, :PANEL])
    squares_part = jnp.einsum("rd,rd->d", gathered, gathered, preferred_element_type=jnp.float32)
    gram_whole, squares_whole = lax.psum((gram_part, squares_part), "dp")
    gram_local = lax.dynamic_slice_in_dim(gram_whole, group_index * columns, columns, 0)
    squares_local = lax.dynamic_slice_in_dim(squares_whole, group_index * columns, columns, 0)
    gram_panel = gram_whole[:PANEL]
    total = jnp.sum(squares_whole)
    scaling = total / D + EPSILON
    panel_held = spread_2(held[:, :PANEL], "dp", 0)
    refitted, change = panel_solve(
        panel_held, mask_from(patterns[0]), gram_panel / scaling, inverse[0]
    )
    normed_local = gram_local / scaling
    correction = lax.dot_general(
        change, normed_local, (((1,), (1,)), ((), ())), precision=lax.Precision.HIGHEST
    )
    adjusted = held.astype(jnp.float32) - correction / (squares_local / scaling + DAMPING)[None, :]
    positions = group_index * columns + jnp.arange(columns, dtype=jnp.int32)
    padded = jnp.pad(refitted, ((0, 0), (0, columns - PANEL)))
    result = jnp.where(positions[None, :] < PANEL, padded, adjusted).astype(jnp.bfloat16)
    pieces = result.reshape(owners, -1, columns)
    spread = lax.all_to_all(pieces, "expert", split_axis=0, concat_axis=0, tiled=True)
    slot_ids = jnp.arange(owners, dtype=jnp.int32)
    source_slot = jnp.sum(
        jnp.where(old_slots[None, :] == new_slots[:, None], slot_ids[None, :], 0), axis=1
    )
    ordered = jnp.take(spread, source_slot, axis=0)
    returned = lax.all_to_all(ordered, "expert", split_axis=0, concat_axis=0, tiled=True)
    return returned.reshape(1, -1, columns)


def solution(mesh):
    placed = (
        P(("dp", "expert"), None),
        P(("dp", "expert"), None),
        P(),
        P(),
        P("expert", None, "dp"),
        P("expert", None, None),
        P("expert", None, None),
    )
    return jax.shard_map(
        shards, mesh=mesh, in_specs=placed, out_specs=P("expert", None, "dp"), check_vma=False
    )
```

profile of v0, /device:TPU:1, one launch (start us, length us, event | category | flops | bytes accessed | tf_op | source)
XLA Modules:
  0.0 445.1 jit_solution(4680424004570815257)
XLA Ops:
  6.5 0.9 compare_reduce_fusion
  7.5 0.2 reduce_window_sum.11
  7.8 0.3 select_reduce_fusion
  8.1 0.3 fusion.7
  8.4 0.1 reshape.75
  8.6 5.2 %gather_fusion = bf16[576,4096]{1,0:T(8,128)(2,1)} fusion(bf16[128,4096]{1,0:T(8,128)(2,1)S(1)} %copy-done, s32[1024]{0:T(1024)S(1)} %pad_clamp_fusion.1), kind=kCustom, calls=%fused_computation | custom fusion | bytes 9439488 | tf_op jit(solution)/shard_map/jit(_take)/gather | solution.py:66
  13.8 8.2 %reshape.74 = bf16[64,9,4096]{2,1,0:T(8,128)(2,1)} reshape(bf16[576,4096]{1,0:T(8,128)(2,1)} %gather_fusion) | data formatting | bytes 9437184 | tf_op jit(solution)/shard_map/jit(_take)/gather | solution.py:66
  22.2 7.4 %select_select_fusion = bf16[64,9,4096]{2,1,0:T(8,128)(2,1)} fusion(bf16[64,9,4096]{2,1,0:T(8,128)(2,1)} %reshape.74, pred[64,9]{1,0:T(8,128)(4,1)S(1)} %copy.24, pred[64,9]{1,0:T(8,128)(4,1)S(1)} %copy.23), kind=kLoop, calls=%fused_computation.4 | loop fusion | flops 4718592 | bytes 9438336 | tf_op jit(solution)/shard_map/jit(_where)/select_n | solution.py:66
  29.6 15.0 %all-to-all-start = ((bf16[64,9,4096]{2,1,0:T(8,128)(2,1)}), bf16[64,9,4096]{2,1,0:T(8,128)(2,1)}, u32[]{:S(2)}, u32[]{:S(2)}) async-start(bf16[64,9,4096]{2,1,0:T(8,128)(2,1)} %select_select_fusion), calls=%async_computation | async-start | bytes 16777216 | tf_op jit(solution)/shard_map/all_to_all | solution.py:67
  44.7 1.8 slice_select_fusion
  46.5 183.9 %all-to-all-done = bf16[64,9,4096]{2,1,0:T(8,128)(2,1)} async-done(((bf16[64,9,4096]{2,1,0:T(8,128)(2,1)}), bf16[64,9,4096]{2,1,0:T(8,128)(2,1)}, u32[]{:S(2)}, u32[]{:S(2)}) %all-to-all-start) | async-done | bytes 4718624 | tf_op jit(solution)/shard_map/all_to_all | solution.py:67
  230.4 8.4 %reshape.70 = bf16[576,4096]{1,0:T(8,128)(2,1)} reshape(bf16[64,9,4096]{2,1,0:T(8,128)(2,1)} %all-to-all-done) | data formatting | bytes 9437184 | tf_op jit(solution)/shard_map/reshape | solution.py:68
  238.8 5.3 %fusion.10 = f32[4096,128]{1,0:T(8,128)} fusion(bf16[576,4096]{1,0:T(8,128)(2,1)} %reshape.70), kind=kOutput, calls=%fused_computation.25 | convolution fusion | flops 603979776 | bytes 6963200 | tf_op jit(solution)/shard_map/dot_general | solution.py:55
  244.3 0.5 copy-done.5
  244.8 0.4 multiply_reduce_fusion
  245.2 0.5 copy.19
  245.7 0.3 reshape.69
  246.0 0.3 copy.26
  246.3 3.4 fusion
  249.7 25.5 %psum.23 = f32[4096]{0:T(1024)S(1)} all-reduce(f32[4096]{0:T(1024)S(1)} %fusion), channel_id=1, replica_groups=mesh['dp'=8,'expert'=64] {'dp'}, use_global_device_ids=true, to_apply=%region_8.9 | all-reduce | flops 4096 | bytes 32768 | tf_op jit(solution)/shard_map/psum | solution.py:71
  275.2 0.6 reduce_sum.44
  276.5 48.8 %all-reduce.6.cloned.1.call-done = f32[4096,128]{1,0:T(8,128)} async-done(((f32[4096,128]{1,0:T(8,128)}), f32[4096,128]{1,0:T(8,128)}) %all-reduce.6.cloned.1.call-update) | async-done | bytes 2097168 | tf_op jit(solution)/shard_map/psum | solution.py:71
  325.3 1.9 fusion.3
  327.2 1.8 fusion.1
  329.0 4.9 %select_convert_fusion = bf16[1536,512]{1,0:T(8,128)(2,1)} fusion(f32[1536,128]{1,0:T(8,128)S(1)} %fusion.1, f32[512]{0:T(512)S(1)} %divide_add_fusion, pred[512]{0:T(512)(128)(4,1)S(1)} %add_compare_fusion, bf16[1536,128]{1,0:T(8,128)(2,1)S(1)} %copy-done.1, f32[4096,128]{1,0:T(8,128)} %all-reduce.6.cloned.1.call-done, s32[]{:T(128)S(6)} %select_n.77, ...), kind=kOutput, calls=%fused_computation.6 | convolution fusion | flops 1212350464 | bytes 5376520 | tf_op jit(solution)/shard_map/dot_general | solution.py:82
  333.9 14.2 %all-to-all-start.1 = ((bf16[64,24,512]{2,1,0:T(8,128)(2,1)}), bf16[64,24,512]{2,1,0:T(8,128)(2,1)S(1)}, u32[]{:S(2)}, u32[]{:S(2)}) async-start(bf16[64,24,512]{2,1,0:T(8,128)(2,1)} %bitcast.28), calls=%async_computation.1 | async-start | bytes 3145728 | tf_op jit(solution)/shard_map/all_to_all | solution.py:90
  348.2 0.2 select_reduce_fusion.1
  348.4 39.6 %all-to-all-done.1 = bf16[64,24,512]{2,1,0:T(8,128)(2,1)S(1)} async-done(((bf16[64,24,512]{2,1,0:T(8,128)(2,1)}), bf16[64,24,512]{2,1,0:T(8,128)(2,1)S(1)}, u32[]{:S(2)}, u32[]{:S(2)}) %all-to-all-start.1) | async-done | bytes 1572896 | tf_op jit(solution)/shard_map/all_to_all | solution.py:90
  388.0 1.8 gather_fusion.1
  389.7 1.6 broadcast_select_fusion
  391.4 45.7 %all_to_all.15 = bf16[64,24,512]{2,1,0:T(8,128)(2,1)S(1)} all-to-all(bf16[64,24,512]{2,1,0:T(8,128)(2,1)S(1)} %broadcast_select_fusion), channel_id=1, replica_groups=mesh['dp'=8,'expert'=64] {'expert'}, dimensions={0} | all-to-all | bytes 3145728 | tf_op jit(solution)/shard_map/all_to_all | solution.py:96
  437.1 1.1 copy.36
  (36 shorter events, 0.9 us)
Async XLA Ops:
  6.5 2.1 copy-start
  29.6 200.8 %all-to-all-start = ((bf16[64,9,4096]{2,1,0:T(8,128)(2,1)}), bf16[64,9,4096]{2,1,0:T(8,128)(2,1)}, u32[]{:S(2)}, u32[]{:S(2)}) async-start(bf16[64,9,4096]{2,1,0:T(8,128)(2,1)} %select_select_fusion), calls=%async_computation | async-start | bytes 16777216 | tf_op jit(solution)/shard_map/all_to_all | solution.py:67
  44.6 231.9 %all-reduce.4.cloned.1.call-start = ((), (), s32[]{:S(2)}) async-start(), calls=%async_computation.3 | async-start | bytes 786432 | tf_op jit(solution)/shard_map/psum | solution.py:21
  46.5 278.8 %all-reduce.6.cloned.1.call-start = ((), (), s32[]{:S(2)}) async-start(), calls=%async_computation.4 | async-start | bytes 4194304 | tf_op jit(solution)/shard_map/psum | solution.py:71
  238.8 5.3 %copy-start.2 = (s32[1,1536,32]{1,2,0:T(8,128)S(1)}, s32[1,1536,32]{1,2,0:T(8,128)}, u32[]{:S(2)}) copy-start(s32[1,1536,32]{1,2,0:T(8,128)} %param.13) | copy-start | bytes 589828
  244.1 0.7 copy-start.5
  246.3 80.9 %copy-start.4 = (f32[1,128,128]{2,1,0:T(8,128)S(1)}, f32[1,128,128]{2,1,0:T(8,128)}, u32[]{:S(2)}) copy-start(f32[1,128,128]{2,1,0:T(8,128)} %param.14) | copy-start | bytes 196612
  276.5 52.5 %copy-start.1 = (bf16[1536,128]{1,0:T(8,128)(2,1)S(1)}, bf16[1536,128]{1,0:T(8,128)(2,1)}, u32[]{:S(2)}) copy-start(bf16[1536,128]{1,0:T(8,128)(2,1)} %all-reduce.4.cloned.1.call-done) | copy-start | bytes 1179652
  325.3 3.7 copy-start.3
  333.9 14.2 %copy-start.6 = (s32[64]{0:T(128)S(1)}, s32[64]{0:T(128)}, u32[]{:S(2)}) copy-start(s32[64]{0:T(128)} %param.10) | copy-start | bytes 772
  333.9 14.3 %copy-start.7 = (s32[64]{0:T(128)S(1)}, s32[64]{0:T(128)}, u32[]{:S(2)}) copy-start(s32[64]{0:T(128)} %param.11) | copy-start | bytes 772
  333.9 54.0 %all-to-all-start.1 = ((bf16[64,24,512]{2,1,0:T(8,128)(2,1)}), bf16[64,24,512]{2,1,0:T(8,128)(2,1)S(1)}, u32[]{:S(2)}, u32[]{:S(2)}) async-start(bf16[64,24,512]{2,1,0:T(8,128)(2,1)} %bitcast.28), calls=%async_computation.1 | async-start | bytes 3145728 | tf_op jit(solution)/shard_map/all_to_all | solution.py:90
Sparse Core Ops, SparseCore 0:
  47.8 75.7 all-reduce.3
  244.3 80.9 all-reduce.5
where the time goes:
time: 446 us; the launch traced here: 445 us
  waiting for transfers between devices  272 us (61%)
  blocking collectives  71.2 us (16%)
  starting transfers between devices  29.3 us (7%)
  local copies, waits for them, and re-layouts  26.9 us (6%)
  other arithmetic  17.2 us (4%)
  between operations  14.3 us (3%)
  matrix products  13.8 us (3%)
    all_to_all x1, waiting for transfers between devices, shards(): lax.all_to_all(outgoing, 'expert', split_axis=0, concat_axis=0, tiled=True)  184 us
    psum x1, waiting for transfers between devices, shards(): gram_whole, squares_whole = lax.psum((gram_part, squares_part), 'dp')  48.8 us
    all_to_all x1, blocking collectives, shards(): lax.all_to_all(ordered, 'expert', split_axis=0, concat_axis=0, tiled=True)  45.7 us
    all_to_all x1, waiting for transfers between devices, shards(): lax.all_to_all(pieces, 'expert', split_axis=0, concat_axis=0, tiled=True)  39.6 us
    psum x1, blocking collectives, shards(): gram_whole, squares_whole = lax.psum((gram_part, squares_part), 'dp')  25.5 us
    all_to_all x1, starting transfers between devices, shards(): lax.all_to_all(outgoing, 'expert', split_axis=0, concat_axis=0, tiled=True)  15 us
    all_to_all x1, starting transfers between devices, shards(): lax.all_to_all(pieces, 'expert', split_axis=0, concat_axis=0, tiled=True)  14.2 us
    gather x2, local copies, waits for them, and re-layouts, shards(): jnp.take(tokens, indices, axis=0)  13.4 us
  transfers between devices with their start and end apart: 4, of which 3 were waited for; matrix products, arithmetic and copies ran while one was open for 5% of the time, Pallas kernels for 0%

commit v1 on v0

v1 whole, which is shorter than its diff:
```python
import jax
import jax.numpy as jnp
from jax import lax
from jax.experimental import pallas as pl
from jax.experimental.pallas import tpu as pltpu
from jax.sharding import Mesh
from jax.sharding import PartitionSpec as P

D = 4096
FF = 1536
PANEL = 128
EPSILON = 1e-06
DAMPING = 0.01
NY, NX, NZ, NC = 8, 4, 8, 2
HELD = 32
ROWS = 168
EXPERT = ("x", "z", "c")
bf16 = jnp.bfloat16
f32 = jnp.float32
HIGHEST = lax.Precision.HIGHEST
VMEM = pl.BlockSpec(memory_space=pltpu.VMEM)
SMEM = pl.BlockSpec(memory_space=pltpu.SMEM)


def prep_kernel(tokens, routes, patterns, inverse, blocks, panel, extra):
    squares = jnp.zeros((128, 128), f32)
    for s in range(32):
        part = tokens[:, s * 128 : (s + 1) * 128]
        blocks[s] = part
        wide = part.astype(f32)
        squares = squares + wide * wide
    panel[0:128, :] = tokens[:, 0:128].astype(f32).T.astype(bf16)
    norms = jnp.sum(squares.T, axis=0, keepdims=True) * (1.0 / D)
    high = norms.astype(bf16).astype(f32)
    named = jnp.concatenate(
        [routes[...].astype(f32), jnp.zeros((128, 120), f32)], axis=1
    ).T
    panel[128:144, :] = jnp.concatenate(
        [named[0:8], high, norms - high, jnp.zeros((6, 128), f32)], axis=0
    ).astype(bf16)
    numbers = patterns[...].astype(f32)
    extra[0:48, :] = jnp.concatenate(
        [numbers[48 * q : 48 * (q + 1)] for q in range(4)], axis=1
    ).astype(bf16)
    rest = inverse[...]
    for q in range(3):
        piece = rest.astype(bf16)
        extra[48 + 16 * q : 64 + 16 * q, :] = piece
        rest = rest - piece.astype(f32)
    extra[96:128, :] = jnp.zeros((32, 128), bf16)


def prepare(tokens, routes, patterns, inverse):
    return pl.pallas_call(
        prep_kernel,
        out_shape=(
            jax.ShapeDtypeStruct((32, 128, 128), bf16),
            jax.ShapeDtypeStruct((144, 128), bf16),
            jax.ShapeDtypeStruct((128, 128), bf16),
        ),
        in_specs=[VMEM] * 4,
        out_specs=(VMEM,) * 3,
        compiler_params=pltpu.CompilerParams(vmem_limit_bytes=16 * 1024 * 1024),
    )(tokens, routes, patterns, inverse)


def gram_kernel(where, wanted, own, other, panels, out, left_all, right, squares, marks, left, total, norms):
    x, c = where[0], where[1]
    ids = wanted[...]
    norms[...] = jnp.zeros_like(norms)
    for half, source in ((0, own), (1, other)):
        core = c if half == 0 else 1 - c

        @pl.loop(0, HELD)
        def _(b):
            place = ((b % NX) * NC + core) * NY + b // NX
            at = pl.ds(pl.multiple_of((half * HELD + b) * 128, 128), 128)
            turned = panels[place, 0:128, :]
            notes = panels[place, 128:144, :].astype(f32)
            left_all[:, at] = turned
            right[at, 128:256] = turned.astype(f32).T.astype(bf16)
            part = source[b]
            right[at, 0:128] = part
            wide = part.astype(f32)
            wide = wide * wide
            high = wide.astype(bf16)
            squares[at, 0:128] = high
            squares[at, 128:256] = (wide - high.astype(f32)).astype(bf16)
            hit = jnp.zeros((HELD, 128), f32)
            for k in range(8):
                hit = jnp.where(notes[k : k + 1, :] == ids, 1.0, hit)
            marks[:, at] = hit
            norms[...] += hit * (notes[8:9, :] + notes[9:10, :])

    chunk = 2048

    @pl.loop(0, 4)
    def _(g):
        @pl.loop(0, 4)
        def _(k):
            at = pl.ds(pl.multiple_of(k * chunk, chunk), chunk)
            hits = marks[pl.ds(pl.multiple_of(g * 8, 8), 8), at]
            for j in range(8):
                row = jnp.broadcast_to(hits[j : j + 1, :], (16, chunk)).astype(bf16)
                for r in range(8):
                    left[j * 128 + r * 16 : j * 128 + r * 16 + 16, :] = (
                        left_all[r * 16 : r * 16 + 16, at] * row
                    )
            product = jnp.dot(left[...], right[at, :], preferred_element_type=f32)

            @pl.when(k == 0)
            def _():
                total[...] = product

            @pl.when(k > 0)
            def _():
                total[...] += product

        for j in range(8):
            out[g * 8 + j, 0:128, :] = total[j * 128 : (j + 1) * 128, 0:128]
            quarter = pl.ds(pl.multiple_of(j * 128 + 32 * x, 32), 32)
            out[g * 8 + j, 128:160, :] = total[quarter, 128:256]

    sums = jnp.dot(marks[...].astype(bf16), squares[...], preferred_element_type=f32)
    sums = sums[:, 0:128] + sums[:, 128:256]
    scale = jnp.broadcast_to(jnp.sum(norms[...], axis=1, keepdims=True), (HELD, 128))
    for e in range(HELD):
        out[e, 160:168, :] = jnp.concatenate(
            [sums[e : e + 1], scale[e : e + 1], jnp.zeros((6, 128), f32)], axis=0
        )


def gram(where, wanted, own, other, panels):
    return pl.pallas_call(
        gram_kernel,
        out_shape=jax.ShapeDtypeStruct((HELD, ROWS, 128), f32),
        in_specs=[SMEM] + [VMEM] * 4,
        out_specs=VMEM,
        scratch_shapes=[
            pltpu.VMEM((128, 8192), bf16),
            pltpu.VMEM((8192, 256), bf16),
            pltpu.VMEM((8192, 256), bf16),
            pltpu.VMEM((HELD, 8192), f32),
            pltpu.VMEM((1024, 2048), bf16),
            pltpu.VMEM((1024, 256), f32),
            pltpu.VMEM((HELD, 128), f32),
        ],
        compiler_params=pltpu.CompilerParams(vmem_limit_bytes=48 * 1024 * 1024),
        cost_estimate=pl.CostEstimate(
            flops=2 * 4096 * 8192 * 256, bytes_accessed=8 << 20, transcendentals=0
        ),
    )(where, wanted, own, other, panels)


def refit_kernel(where, sums, shared, held, out, normed, scaled, inverse):
    y = where[2]
    scaling = sums[0, 161:162, :] + EPSILON
    for q in range(NX):
        diagonal = sums[q, 160:161, :] / scaling + DAMPING
        scaled[:, q * 128 : (q + 1) * 128] = sums[q, 0:128, :] / scaling / diagonal
        normed[q * 32 : (q + 1) * 32, :] = sums[q, 128:160, :] / scaling
    a = lax.broadcasted_iota(jnp.int32, (128, 128), 0)
    b = lax.broadcasted_iota(jnp.int32, (128, 128), 1)
    normed[...] += jnp.where(a == b, DAMPING, 0.0)
    for q in range(NY):
        inverse[q * 16 : (q + 1) * 16, :] = (
            shared[q, 240:256, :].astype(f32)
            + shared[q, 256:272, :].astype(f32)
            + shared[q, 272:288, :].astype(f32)
        )

    @pl.loop(0, NY)
    def _(q):
        numbers = shared[q, 192:240, :]
        spread = []
        for part in range(4):
            pick = jnp.where(a == part * 32 + b // 4, 1.0, 0.0).astype(bf16)
            spread.append(jnp.dot(numbers, pick, preferred_element_type=f32))
        number = jnp.concatenate(spread, axis=0)
        lane = lax.broadcasted_iota(jnp.int32, (192, 128), 1) % 4
        code = number.astype(jnp.int32)
        kept = jnp.where(lane == 0, 0b000111, jnp.where(lane == 1, 0b011001, jnp.where(lane == 2, 0b101010, 0b110100)))
        mask = ((kept >> code) & 1).astype(f32)
        panel = shared[q, 0:192, :].astype(f32)
        dropped = (1.0 - mask) * panel
        step = jnp.dot(dropped, normed[...], precision=HIGHEST, preferred_element_type=f32)
        step = jnp.dot(step, inverse[...], precision=HIGHEST, preferred_element_type=f32)
        refitted = mask * (panel + step)
        change = refitted - panel
        correction = jnp.dot(change, scaled[...], precision=HIGHEST, preferred_element_type=f32)
        rows = pl.ds(pl.multiple_of(q * 192, 64), 192)
        for k in range(4):
            for half in range(2):
                piece = held[16 * k + 2 * q + half, 0:96, :].astype(f32)
                fixed = piece - correction[half * 96 : (half + 1) * 96, k * 128 : (k + 1) * 128]
                out[pl.ds(pl.multiple_of(q * 192 + half * 96, 32), 96), k * 128 : (k + 1) * 128] = fixed.astype(bf16)

        @pl.when(y == 0)
        def _():
            out[rows, 0:128] = refitted.astype(bf16)


def refit(where, sums, shared, held):
    return pl.pallas_call(
        refit_kernel,
        out_shape=jax.ShapeDtypeStruct((FF, 512), bf16),
        in_specs=[SMEM] + [VMEM] * 3,
        out_specs=VMEM,
        scratch_shapes=[
            pltpu.VMEM((128, 128), f32),
            pltpu.VMEM((128, 512), f32),
            pltpu.VMEM((128, 128), f32),
        ],
        compiler_params=pltpu.CompilerParams(vmem_limit_bytes=32 * 1024 * 1024),
    )(where, sums, shared, held)


def swap(value, axis, size, step):
    return lax.ppermute(value, axis, [(i, (i + step) % size) for i in range(size)])


def after(value, *others):
    return lax.optimization_barrier((value, *others))[0]


def shards(tokens, routes, old_slots, new_slots, weights, patterns, inverse):
    x, y, z, c = (lax.axis_index(name) for name in ("x", "y", "z", "c"))
    me = (x * NZ + z) * NC + c
    where = jnp.stack([x, c, y]).astype(jnp.int32)
    slot = jnp.arange(64, dtype=jnp.int32)
    source = jnp.sum(jnp.where(old_slots[None, :] == new_slots[:, None], slot[None, :], 0), axis=1)
    order = new_slots.reshape(NX, NZ, NC).transpose(2, 1, 0).reshape(NC, HELD)
    wanted = jnp.broadcast_to(
        lax.dynamic_index_in_dim(order, c, 0, keepdims=False)[:, None], (HELD, 128)
    ).astype(f32)

    blocks, panel, extra = prepare(
        tokens,
        routes,
        lax.dynamic_slice_in_dim(patterns[0], y * 192, 192, 0),
        lax.dynamic_slice_in_dim(inverse[0], y * 16, 16, 0),
    )
    panels = lax.all_gather(panel, "y", axis=0, tiled=False)
    panels = lax.all_gather(panels, ("x", "c"), axis=0, tiled=False).reshape(64, 144, 128)
    own = lax.all_to_all(blocks, ("y", "x"), 0, 0, tiled=True)
    other = swap(own, "c", NC, 1)

    pieces = weights[0].reshape(16, 96, 4, 128).transpose(2, 0, 1, 3).reshape(64, 96, 128)
    tail = jnp.pad(extra.reshape(64, 2, 128), ((0, 0), (0, 6), (0, 0)))
    pieces = jnp.concatenate([pieces, tail], axis=1)
    pieces = after(pieces, own)
    spread = lax.all_to_all(pieces, EXPERT, 0, 0, tiled=True)
    spread = jnp.take(spread, source, axis=0, mode="clip")
    held = lax.all_to_all(spread, EXPERT, 0, 0, tiled=True)

    sums = gram(where, wanted, own, other, panels)
    sums = lax.psum_scatter(sums, "z", scatter_dimension=0, tiled=True)
    sums = lax.all_to_all(sums, "x", 0, 0, tiled=True)

    moved = held[0:16, 0:96].reshape(NY, 192, 128)
    moved = lax.all_to_all(moved, "y", 0, 0, tiled=True)[0]
    shared = jnp.concatenate([moved, held[:, 96:98].reshape(128, 128)[0:96]], axis=0)
    shared = lax.all_gather(shared, "y", axis=0, tiled=False)
    return refit(where, sums, shared, held)[None]


def solution(mesh):
    grid = Mesh(mesh.devices.reshape(NY, NX, NZ, NC), ("y", "x", "z", "c"))
    placed = (
        P(("y", "x", "z", "c"), None),
        P(("y", "x", "z", "c"), None),
        P(),
        P(),
        P(EXPERT, None, "y"),
        P(EXPERT, None, None),
        P(EXPERT, None, None),
    )
    return jax.shard_map(
        shards, mesh=grid, in_specs=placed, out_specs=P(EXPERT, None, "y"), check_vma=False
    )
```

time: 446 us -> 272 us (0.61)
  the two profiles are of different devices: /device:TPU:1 before, /device:TPU:2 now
where the time goes in v1:
time: 272 us; the launch traced here: 271 us
  blocking collectives  152 us (56%)
  Pallas kernels  43.7 us (16%)
  starting transfers between devices  24.4 us (9%)
  waiting for transfers between devices  20.2 us (7%)
  local copies, waits for them, and re-layouts  15.1 us (6%)
  between operations  13.5 us (5%)
    all_to_all x1, blocking collectives, shards(): held = lax.all_to_all(spread, EXPERT, 0, 0, tiled=True)  67.9 us
    pallas_call x1, Pallas kernels, gram(): pl.pallas_call(gram_kernel, out_shape=jax.ShapeDtypeStruct((HELD, ROWS, 1...  32.4 us
    all_to_all x1, blocking collectives, shards(): own = lax.all_to_all(blocks, ('y', 'x'), 0, 0, tiled=True)  30.4 us
    all_gather x1, blocking collectives, shards(): panels = lax.all_gather(panel, 'y', axis=0, tiled=False)  28.6 us
    all_gather x1, blocking collectives, shards(): shared = lax.all_gather(shared, 'y', axis=0, tiled=False)  25.6 us
    all_to_all x1, waiting for transfers between devices, shards(): moved = lax.all_to_all(moved, 'y', 0, 0, tiled=True)[0]  14.3 us
    all_to_all x1, starting transfers between devices, shards(): spread = lax.all_to_all(pieces, EXPERT, 0, 0, tiled=True)  14.2 us
    pallas_call x1, Pallas kernels, refit(): pl.pallas_call(refit_kernel, out_shape=jax.ShapeDtypeStruct((FF, 512), bf...  10.9 us
  transfers between devices with their start and end apart: 6, of which 2 were waited for; matrix products, arithmetic and copies ran while one was open for 4% of the time, Pallas kernels for 12%

profile of v1, /device:TPU:2, one launch (start us, length us, event | category | flops | bytes accessed | tf_op | source)
XLA Modules:
  0.0 271.0 jit_solution(8370279288474813229)
XLA Ops:
  6.5 0.8 copy.24.routes
  7.4 0.1 copy-done
  7.5 0.1 constant_dynamic-slice_fusion
  7.6 0.1 copy.23
  7.7 0.7 dynamic-slice_bitcast_fusion.inverse
  8.4 1.2 copy-done.1
  9.6 0.5 shard_map.73
  10.0 28.6 %all-gather = bf16[1152,128]{1,0:T(8,128)(2,1)} all-gather(bf16[144,128]{1,0:T(8,128)(2,1)S(1)} %get-tuple-element.10), channel_id=2, replica_groups=mesh['y'=8,'x'=4,'z'=8,'c'=2] {'y'}, dimensions={0}, use_global_device_ids=true | all-gather | bytes 331776 | tf_op jit(solution)/shard_map/all_gather | solution.py:243
  38.7 30.4 %all_to_all.25.own = bf16[32,128,128]{2,1,0:T(8,128)(2,1)S(1)} all-to-all(bf16[32,128,128]{2,1,0:T(8,128)(2,1)S(1)} %get-tuple-element.9), channel_id=1, replica_groups=mesh['y'=8,'x'=4,'z'=8,'c'=2] {'y','x'}, dimensions={0} | all-to-all | bytes 2097152 | tf_op jit(solution)/shard_map/all_to_all | solution.py:245
  69.0 1.9 collective-permute-start
  70.9 3.5 %reshape_squeeze.3 = bf16[16,96,4,128]{3,2,1,0:T(4,128)(2,1)} reshape(bf16[1,1536,512]{2,1,0:T(8,128)(2,1)} %param.11) | data formatting | bytes 3145728 | tf_op jit(solution)/shard_map/reshape;squeeze | solution.py:248
  74.4 1.6 copy.25
  76.0 1.3 fusion.1
  77.4 14.2 %all-to-all-start.2 = ((bf16[64,104,128]{2,1,0:T(8,128)(2,1)}), bf16[64,104,128]{2,1,0:T(8,128)(2,1)}, u32[]{:S(2)}, u32[]{:S(2)}) async-start(bf16[64,104,128]{2,1,0:T(8,128)(2,1)} %fusion.1), calls=%async_computation.3 | async-start | bytes 3407872 | tf_op jit(solution)/shard_map/all_to_all | solution.py:252
  91.7 0.1 reshape.27
  91.8 0.1 copy.22
  91.9 0.1 reshape.28
  92.0 0.1 pad_add_fusion.where
  92.1 0.1 broadcast_in_dim.28.wanted
  92.2 1.7 copy-done.2
  93.9 32.4 %shard_map.74 = f32[32,168,128]{2,1,0:T(8,128)} custom-call(s32[3]{0:T(128)S(1)} %pad_add_fusion.where, f32[32,128]{1,0:T(8,128)S(1)} %broadcast_in_dim.28.wanted, bf16[32,128,128]{2,1,0:T(8,128)(2,1)S(1)} %all_to_all.25.own, bf16[32,128,128]{2,1,0:T(8,128)(2,1)S(1)} %collective-permute-done.other, bf16[64,144,128]{2,1,0:T(8,128)(2,1)S(1)} %copy-done.2), custom_call_target="tpu_custom_call" | custom-call | flops 17179869184 | bytes 8388608 | tf_op jit(solution)/shard_map/pallas_call | solution.py:134
  126.2 0.6 copy-done.4
  126.9 0.2 select_reduce_fusion
  127.1 5.8 %all-to-all-done.2 = bf16[64,104,128]{2,1,0:T(8,128)(2,1)} async-done(((bf16[64,104,128]{2,1,0:T(8,128)(2,1)}), bf16[64,104,128]{2,1,0:T(8,128)(2,1)}, u32[]{:S(2)}, u32[]{:S(2)}) %all-to-all-start.2) | async-done | bytes 1703968 | tf_op jit(solution)/shard_map/all_to_all | solution.py:252
  132.9 3.4 %gather_fusion = bf16[64,104,128]{2,1,0:T(8,128)(2,1)} fusion(bf16[64,104,128]{2,1,0:T(8,128)(2,1)} %all-to-all-done.2, s32[1024]{0:T(1024)S(1)} %pad_clamp_fusion), kind=kCustom, calls=%fused_computation | custom fusion | bytes 3408128 | tf_op jit(solution)/shard_map/jit(_take)/gather | solution.py:253
  136.3 67.9 %all_to_all.26.held = bf16[64,104,128]{2,1,0:T(8,128)(2,1)S(1)} all-to-all(bf16[64,104,128]{2,1,0:T(8,128)(2,1)} %gather_fusion), channel_id=1, replica_groups=mesh['y'=8,'x'=4,'z'=8,'c'=2] {'x','z','c'}, dimensions={0} | all-to-all | bytes 3407872 | tf_op jit(solution)/shard_map/all_to_all | solution.py:254
  204.3 0.8 slice.20
  205.1 3.5 %all-to-all-start.4 = ((bf16[8,192,128]{2,1,0:T(8,128)(2,1)}), bf16[8,192,128]{2,1,0:T(8,128)(2,1)S(1)}, u32[]{:S(2)}, u32[]{:S(2)}) async-start(bf16[8,192,128]{2,1,0:T(8,128)(2,1)} %bitcast.11), calls=%async_computation.5 | async-start | bytes 786432 | tf_op jit(solution)/shard_map/all_to_all | solution.py:261
  208.5 14.3 %all-to-all-done.4 = bf16[8,192,128]{2,1,0:T(8,128)(2,1)S(1)} async-done(((bf16[8,192,128]{2,1,0:T(8,128)(2,1)}), bf16[8,192,128]{2,1,0:T(8,128)(2,1)S(1)}, u32[]{:S(2)}, u32[]{:S(2)}) %all-to-all-start.4) | async-done | bytes 393248 | tf_op jit(solution)/shard_map/all_to_all | solution.py:261
  222.9 4.8 %all-to-all-start.1 = ((f32[4,168,128]{2,1,0:T(8,128)}), f32[4,168,128]{2,1,0:T(8,128)S(1)}, u32[]{:S(2)}, u32[]{:S(2)}) async-start(f32[4,168,128]{2,1,0:T(8,128)} %reduce-scatter.2.cloned.1.call-done), calls=%async_computation.2 | async-start | bytes 688128 | tf_op jit(solution)/shard_map/all_to_all | solution.py:258
  227.7 25.6 %all-gather.2 = bf16[2304,128]{1,0:T(8,128)(2,1)S(1)} all-gather(bf16[288,128]{1,0:T(8,128)(2,1)S(1)} %pad_maximum_fusion), channel_id=4, replica_groups=mesh['y'=8,'x'=4,'z'=8,'c'=2] {'y'}, dimensions={0}, use_global_device_ids=true | all-gather | bytes 663552 | tf_op jit(solution)/shard_map/all_gather | solution.py:263
  253.3 10.9 %shard_map.75 = bf16[1536,512]{1,0:T(8,128)(2,1)} custom-call(s32[3]{0:T(128)S(1)} %pad_add_fusion.where, f32[4,168,128]{2,1,0:T(8,128)S(1)} %all-to-all-done.1.sums, bf16[8,288,128]{2,1,0:T(8,128)(2,1)S(1)} %bitcast.19, bf16[64,104,128]{2,1,0:T(8,128)(2,1)S(1)} %all_to_all.26.held), custom_call_target="tpu_custom_call" | custom-call | tf_op jit(solution)/shard_map/pallas_call | solution.py:204
  (19 shorter events, 0.2 us)
Async XLA Ops:
  6.5 0.9 copy-start
  6.5 85.6 %all-gather.5.cloned.1.call-start = ((), (), s32[]{:S(2)}) async-start(), calls=%async_computation.7 | async-start | bytes 2654208 | tf_op jit(solution)/shard_map/all_gather | solution.py:244
  8.4 1.2 copy-start.1
  69.0 23.1 %collective-permute-start = (bf16[32,128,128]{2,1,0:T(8,128)(2,1)S(1)}, bf16[32,128,128]{2,1,0:T(8,128)(2,1)S(1)}, u32[]{:S(2)}, u32[]{:S(2)}) collective-permute-start(bf16[32,128,128]{2,1,0:T(8,128)(2,1)S(1)} %all_to_all.25.own), channel_id=1, source_target_pairs={{0,1},{1,0},{2,3},{3,2},{4,5},{5,4},{6,7},{7,6},{8,9},{9,8},{10,11... | collective-permute-start | bytes 3145736 | tf_op jit(solution)/shard_map/ppermute | solution.py:219
  77.4 14.3 %copy-start.3 = (s32[64]{0:T(128)S(1)}, s32[64]{0:T(128)}, u32[]{:S(2)}) copy-start(s32[64]{0:T(128)} %param.10) | copy-start | bytes 772
  77.4 55.5 %all-to-all-start.2 = ((bf16[64,104,128]{2,1,0:T(8,128)(2,1)}), bf16[64,104,128]{2,1,0:T(8,128)(2,1)}, u32[]{:S(2)}, u32[]{:S(2)}) async-start(bf16[64,104,128]{2,1,0:T(8,128)(2,1)} %fusion.1), calls=%async_computation.3 | async-start | bytes 3407872 | tf_op jit(solution)/shard_map/all_to_all | solution.py:252
  91.6 131.2 %reduce-scatter.2.cloned.1.call-start = ((), (), s32[]{:S(2)}) async-start(), calls=%async_computation.6 | async-start | bytes 3096576 | tf_op jit(solution)/shard_map/reduce_scatter | solution.py:257
  92.2 1.7 copy-start.2
  126.2 0.7 copy-start.4
  205.1 17.8 %all-to-all-start.4 = ((bf16[8,192,128]{2,1,0:T(8,128)(2,1)}), bf16[8,192,128]{2,1,0:T(8,128)(2,1)S(1)}, u32[]{:S(2)}, u32[]{:S(2)}) async-start(bf16[8,192,128]{2,1,0:T(8,128)(2,1)} %bitcast.11), calls=%async_computation.5 | async-start | bytes 786432 | tf_op jit(solution)/shard_map/all_to_all | solution.py:261
  222.9 30.4 %all-to-all-start.1 = ((f32[4,168,128]{2,1,0:T(8,128)}), f32[4,168,128]{2,1,0:T(8,128)S(1)}, u32[]{:S(2)}, u32[]{:S(2)}) async-start(f32[4,168,128]{2,1,0:T(8,128)} %reduce-scatter.2.cloned.1.call-done), calls=%async_computation.2 | async-start | bytes 688128 | tf_op jit(solution)/shard_map/all_to_all | solution.py:258
Sparse Core Ops, SparseCore 0:
  38.8 35.6 all-gather.4
  126.4 78.0 reduce-scatter.1

commit v2 on v1

--- a/solution.py
+++ b/solution.py
@@ -17,55 +17,100 @@
 EXPERT = ("x", "z", "c")
 bf16 = jnp.bfloat16
 f32 = jnp.float32
-HIGHEST = lax.Precision.HIGHEST
 VMEM = pl.BlockSpec(memory_space=pltpu.VMEM)
 SMEM = pl.BlockSpec(memory_space=pltpu.SMEM)
 
 
-def prep_kernel(tokens, routes, patterns, inverse, blocks, panel, extra):
+def sort_kernel(where, *refs):
+    came, (panels, rows) = refs[:NY], refs[NY:]
+    for s in range(NY):
+        panels[s * 144 : (s + 1) * 144, :] = came[s][0:144, :]
+
+        @pl.when(where[2] == s)
+        def _(s=s):
+            rows[...] = came[s][144:336, :].astype(f32)
+
+
+def sort(where, came):
+    return pl.pallas_call(
+        sort_kernel,
+        out_shape=(
+            jax.ShapeDtypeStruct((NY * 144, 128), bf16),
+            jax.ShapeDtypeStruct((192, 128), f32),
+        ),
+        in_specs=[SMEM] + [VMEM] * NY,
+        out_specs=(VMEM,) * 2,
+        compiler_params=pltpu.CompilerParams(vmem_limit_bytes=16 * 1024 * 1024),
+    )(where, *came)
+
+
+def pack_kernel(weights, patterns, inverse, rows, pieces):
+    numbers = patterns[...].astype(f32)
+    rest = inverse[...]
+    parts = []
+    for q in range(3):
+        piece = rest.astype(bf16).astype(f32)
+        parts.append(piece)
+        rest = rest - piece
+    extra = jnp.concatenate(
+        [numbers[48 * q : 48 * (q + 1)] for q in range(4)], axis=1
+    )
+    extra = jnp.concatenate([extra] + parts + [jnp.zeros((32, 128), f32)], axis=0)
+    for p in range(64):
+        k, q = p // 16, p % 16
+        pieces[p, 0:96, :] = weights[96 * q : 96 * (q + 1), 128 * k : 128 * (k + 1)]
+        pieces[p, 96:104, :] = jnp.concatenate(
+            [extra[2 * p : 2 * p + 2], rows[3 * p : 3 * p + 3, :], jnp.zeros((3, 128), f32)], axis=0
+        ).astype(bf16)
+
+
+def pack(weights, patterns, inverse, rows):
+    return pl.pallas_call(
+        pack_kernel,
+        out_shape=jax.ShapeDtypeStruct((64, 104, 128), bf16),
+        in_specs=[VMEM] * 4,
+        out_specs=VMEM,
+        compiler_params=pltpu.CompilerParams(vmem_limit_bytes=16 * 1024 * 1024),
+    )(weights, patterns, inverse, rows)
+
+
+def prep_kernel(tokens, routes, rows, blocks, notes):
     squares = jnp.zeros((128, 128), f32)
     for s in range(32):
         part = tokens[:, s * 128 : (s + 1) * 128]
         blocks[s] = part
         wide = part.astype(f32)
         squares = squares + wide * wide
-    panel[0:128, :] = tokens[:, 0:128].astype(f32).T.astype(bf16)
+    turned = tokens[:, 0:128].astype(f32).T.astype(bf16)
     norms = jnp.sum(squares.T, axis=0, keepdims=True) * (1.0 / D)
     high = norms.astype(bf16).astype(f32)
     named = jnp.concatenate(
         [routes[...].astype(f32), jnp.zeros((128, 120), f32)], axis=1
     ).T
-    panel[128:144, :] = jnp.concatenate(
+    facts = jnp.concatenate(
         [named[0:8], high, norms - high, jnp.zeros((6, 128), f32)], axis=0
     ).astype(bf16)
-    numbers = patterns[...].astype(f32)
-    extra[0:48, :] = jnp.concatenate(
-        [numbers[48 * q : 48 * (q + 1)] for q in range(4)], axis=1
-    ).astype(bf16)
-    rest = inverse[...]
-    for q in range(3):
-        piece = rest.astype(bf16)
-        extra[48 + 16 * q : 64 + 16 * q, :] = piece
-        rest = rest - piece.astype(f32)
-    extra[96:128, :] = jnp.zeros((32, 128), bf16)
-
-
-def prepare(tokens, routes, patterns, inverse):
+    for s in range(NY):
+        notes[s, 0:128, :] = turned
+        notes[s, 128:144, :] = facts
+        notes[s, 144:336, :] = rows[s * 192 : (s + 1) * 192, :]
+
+
+def prepare(tokens, routes, rows):
     return pl.pallas_call(
         prep_kernel,
         out_shape=(
             jax.ShapeDtypeStruct((32, 128, 128), bf16),
-            jax.ShapeDtypeStruct((144, 128), bf16),
-            jax.ShapeDtypeStruct((128, 128), bf16),
+            jax.ShapeDtypeStruct((NY, 336, 128), bf16),
         ),
-        in_specs=[VMEM] * 4,
-        out_specs=(VMEM,) * 3,
+        in_specs=[VMEM] * 3,
+        out_specs=(VMEM,) * 2,
         compiler_params=pltpu.CompilerParams(vmem_limit_bytes=16 * 1024 * 1024),
-    )(tokens, routes, patterns, inverse)
+    )(tokens, routes, rows)
 
 
 def gram_kernel(where, wanted, own, other, panels, out, left_all, right, squares, marks, left, total, norms):
-    x, c = where[0], where[1]
+    x, c, y = where[0], where[1], where[2]
     ids = wanted[...]
     norms[...] = jnp.zeros_like(norms)
     for half, source in ((0, own), (1, other)):
@@ -73,7 +118,7 @@
 
         @pl.loop(0, HELD)
         def _(b):
-            place = ((b % NX) * NC + core) * NY + b // NX
+            place = ((b % NX) * NC + core) * NY + lax.rem(y - b // NX + NY, NY)
             at = pl.ds(pl.multiple_of((half * HELD + b) * 128, 128), 128)
             turned = panels[place, 0:128, :]
             notes = panels[place, 128:144, :].astype(f32)
@@ -152,22 +197,37 @@
     )(where, wanted, own, other, panels)
 
 
-def refit_kernel(where, sums, shared, held, out, normed, scaled, inverse):
-    y = where[2]
-    scaling = sums[0, 161:162, :] + EPSILON
-    for q in range(NX):
-        diagonal = sums[q, 160:161, :] / scaling + DAMPING
-        scaled[:, q * 128 : (q + 1) * 128] = sums[q, 0:128, :] / scaling / diagonal
-        normed[q * 32 : (q + 1) * 32, :] = sums[q, 128:160, :] / scaling
+def parts_of(value, count):
+    found = []
+    for _ in range(count):
+        part = value.astype(bf16)
+        found.append(part)
+        value = value - part.astype(f32)
+    return found
+
+
+def refit_kernel(where, s0, s1, s2, s3, shared, held, out, normed, scaled, inverse):
+    x, y = where[0], where[2]
+    scaling = s0[161:162, :] + EPSILON
     a = lax.broadcasted_iota(jnp.int32, (128, 128), 0)
     b = lax.broadcasted_iota(jnp.int32, (128, 128), 1)
-    normed[...] += jnp.where(a == b, DAMPING, 0.0)
+    for step, sums in enumerate((s0, s1, s2, s3)):
+        q = lax.rem(x - step + NX, NX)
+        diagonal = sums[160:161, :] / scaling + DAMPING
+        high, low = parts_of(sums[0:128, :] / scaling / diagonal, 2)
+        at = pl.ds(pl.multiple_of(q * 128, 128), 128)
+        scaled[0:128, at] = high
+        scaled[128:256, at] = low
+        scaled[256:384, at] = high
+        rows = lax.broadcasted_iota(jnp.int32, (32, 128), 0) + q * 32
+        lanes = lax.broadcasted_iota(jnp.int32, (32, 128), 1)
+        damped = sums[128:160, :] / scaling + jnp.where(rows == lanes, DAMPING, 0.0)
+        for k, part in enumerate(parts_of(damped, 3)):
+            normed[pl.ds(pl.multiple_of(k * 128 + q * 32, 32), 32), :] = part
     for q in range(NY):
-        inverse[q * 16 : (q + 1) * 16, :] = (
-            shared[q, 240:256, :].astype(f32)
-            + shared[q, 256:272, :].astype(f32)
-            + shared[q, 272:288, :].astype(f32)
-        )
+        part = [shared[q, 240 + 16 * k : 256 + 16 * k, :] for k in range(3)]
+        for k, source in enumerate((0, 1, 0, 2, 1, 0)):
+            inverse[k * 128 + q * 16 : k * 128 + q * 16 + 16, :] = part[source]
 
     @pl.loop(0, NY)
     def _(q):
@@ -182,37 +242,43 @@
         kept = jnp.where(lane == 0, 0b000111, jnp.where(lane == 1, 0b011001, jnp.where(lane == 2, 0b101010, 0b110100)))
         mask = ((kept >> code) & 1).astype(f32)
         panel = shared[q, 0:192, :].astype(f32)
-        dropped = (1.0 - mask) * panel
-        step = jnp.dot(dropped, normed[...], precision=HIGHEST, preferred_element_type=f32)
-        step = jnp.dot(step, inverse[...], precision=HIGHEST, preferred_element_type=f32)
+        dropped = ((1.0 - mask) * panel).astype(bf16)
+        step = jnp.dot(jnp.concatenate([dropped] * 3, axis=1), normed[...], preferred_element_type=f32)
+        high, middle, low = parts_of(step, 3)
+        step = jnp.dot(
+            jnp.concatenate([high, high, middle, high, middle, low], axis=1),
+            inverse[...],
+            preferred_element_type=f32,
+        )
         refitted = mask * (panel + step)
-        change = refitted - panel
-        correction = jnp.dot(change, scaled[...], precision=HIGHEST, preferred_element_type=f32)
-        rows = pl.ds(pl.multiple_of(q * 192, 64), 192)
+        high, low = parts_of(refitted - panel, 2)
+        correction = jnp.dot(
+            jnp.concatenate([high, high, low], axis=1), scaled[...], preferred_element_type=f32
+        )
         for k in range(4):
             for half in range(2):
-                piece = held[16 * k + 2 * q + half, 0:96, :].astype(f32)
+                piece = held[16 * k + 2 * q + half, :, :].astype(f32)
                 fixed = piece - correction[half * 96 : (half + 1) * 96, k * 128 : (k + 1) * 128]
                 out[pl.ds(pl.multiple_of(q * 192 + half * 96, 32), 96), k * 128 : (k + 1) * 128] = fixed.astype(bf16)
 
         @pl.when(y == 0)
         def _():
-            out[rows, 0:128] = refitted.astype(bf16)
+            out[pl.ds(pl.multiple_of(q * 192, 64), 192), 0:128] = refitted.astype(bf16)
 
 
 def refit(where, sums, shared, held):
     return pl.pallas_call(
         refit_kernel,
         out_shape=jax.ShapeDtypeStruct((FF, 512), bf16),
-        in_specs=[SMEM] + [VMEM] * 3,
+        in_specs=[SMEM] + [VMEM] * 6,
         out_specs=VMEM,
         scratch_shapes=[
-            pltpu.VMEM((128, 128), f32),
-            pltpu.VMEM((128, 512), f32),
-            pltpu.VMEM((128, 128), f32),
+            pltpu.VMEM((384, 128), bf16),
+            pltpu.VMEM((384, 512), bf16),
+            pltpu.VMEM((768, 128), bf16),
         ],
         compiler_params=pltpu.CompilerParams(vmem_limit_bytes=32 * 1024 * 1024),
-    )(where, sums, shared, held)
+    )(where, *sums, shared, held)
 
 
 def swap(value, axis, size, step):
@@ -234,33 +300,41 @@
         lax.dynamic_index_in_dim(order, c, 0, keepdims=False)[:, None], (HELD, 128)
     ).astype(f32)
 
-    blocks, panel, extra = prepare(
-        tokens,
-        routes,
+    blocks, notes = prepare(tokens, routes, weights[0, :, 0:PANEL])
+    own = lax.all_to_all(blocks, ("y", "x"), 0, 0, tiled=True)
+
+    def note(step):
+        return lax.dynamic_index_in_dim(notes, (y + step) % NY, 0, keepdims=False)
+
+    came = [note(0)] + [swap(note(step), "y", NY, step) for step in range(1, NY)]
+    own, *came = lax.optimization_barrier((own, *came))
+    panels, rows = sort(where, came)
+    panels = lax.all_gather(panels, ("x", "c"), axis=0, tiled=False).reshape(64, 144, 128)
+    pieces = pack(
+        weights[0],
         lax.dynamic_slice_in_dim(patterns[0], y * 192, 192, 0),
         lax.dynamic_slice_in_dim(inverse[0], y * 16, 16, 0),
-    )
-    panels = lax.all_gather(panel, "y", axis=0, tiled=False)
-    panels = lax.all_gather(panels, ("x", "c"), axis=0, tiled=False).reshape(64, 144, 128)
-    own = lax.all_to_all(blocks, ("y", "x"), 0, 0, tiled=True)
+        rows,
+    )
+    spread = lax.all_to_all(pieces, EXPERT, 0, 0, tiled=True)
     other = swap(own, "c", NC, 1)
-
-    pieces = weights[0].reshape(16, 96, 4, 128).transpose(2, 0, 1, 3).reshape(64, 96, 128)
-    tail = jnp.pad(extra.reshape(64, 2, 128), ((0, 0), (0, 6), (0, 0)))
-    pieces = jnp.concatenate([pieces, tail], axis=1)
-    pieces = after(pieces, own)
-    spread = lax.all_to_all(pieces, EXPERT, 0, 0, tiled=True)
-    spread = jnp.take(spread, source, axis=0, mode="clip")
-    held = lax.all_to_all(spread, EXPERT, 0, 0, tiled=True)
+    tails = jnp.take(spread[:, 96:104], source, axis=0, mode="clip")
+    tails = lax.all_to_all(tails, EXPERT, 0, 0, tiled=True)
+    shared = jnp.concatenate(
+        [tails[:, 2:5].reshape(192, 128), tails[:, 0:2].reshape(128, 128)[0:96]], axis=0
+    )
+    shared = lax.all_gather(shared, "y", axis=0, tiled=False)
+    held = jnp.take(spread[:, 0:96], source, axis=0, mode="clip")
+    held = lax.all_to_all(after(held, tails), EXPERT, 0, 0, tiled=True)
 
     sums = gram(where, wanted, own, other, panels)
     sums = lax.psum_scatter(sums, "z", scatter_dimension=0, tiled=True)
-    sums = lax.all_to_all(sums, "x", 0, 0, tiled=True)
-
-    moved = held[0:16, 0:96].reshape(NY, 192, 128)
-    moved = lax.all_to_all(moved, "y", 0, 0, tiled=True)[0]
-    shared = jnp.concatenate([moved, held[:, 96:98].reshape(128, 128)[0:96]], axis=0)
-    shared = lax.all_gather(shared, "y", axis=0, tiled=False)
+    sums = after(sums, shared)
+
+    def column(step):
+        return lax.dynamic_index_in_dim(sums, (x + step) % NX, 0, keepdims=False)
+
+    sums = [column(0)] + [swap(column(step), "x", NX, step) for step in range(1, NX)]
     return refit(where, sums, shared, held)[None]
 
 

time: 272 us -> 254 us (0.934)
  the two profiles are of different devices: /device:TPU:2 before, /device:TPU:1 now
where the time goes in v2:
time: 254 us; the launch traced here: 250 us
  starting transfers between devices  84.4 us (33%)
  waiting for transfers between devices  63.7 us (25%)
  Pallas kernels  45.1 us (18%)
  blocking collectives  27.4 us (11%)
  local copies, waits for them, and re-layouts  15.2 us (6%)
  between operations  13.9 us (5%)
    ppermute x11, starting transfers between devices, swap(): lax.ppermute(value, axis, [(i, (i + step) % size) for i in range(size)])  42.4 us
    pallas_call x1, Pallas kernels, gram(): pl.pallas_call(gram_kernel, out_shape=jax.ShapeDtypeStruct((HELD, ROWS, 1...  33.2 us
    all_gather x1, blocking collectives, shards(): shared = lax.all_gather(shared, 'y', axis=0, tiled=False)  27.4 us
    reduce_scatter x1, waiting for transfers between devices, shards(): sums = lax.psum_scatter(sums, 'z', scatter_dimension=0, tiled=True)  23.4 us
    all_gather x1, waiting for transfers between devices, shards(): lax.all_gather(panels, ('x', 'c'), axis=0, tiled=False)  19.1 us
    ppermute x11, waiting for transfers between devices, swap(): lax.ppermute(value, axis, [(i, (i + step) % size) for i in range(size)])  14.3 us
    all_to_all x1, starting transfers between devices, shards(): spread = lax.all_to_all(pieces, EXPERT, 0, 0, tiled=True)  13.7 us
    all_to_all x1, starting transfers between devices, shards(): tails = lax.all_to_all(tails, EXPERT, 0, 0, tiled=True)  12.9 us
  transfers between devices with their start and end apart: 17, of which 7 were waited for; matrix products, arithmetic and copies ran while one was open for 4% of the time, Pallas kernels for 14%

profile of v2, /device:TPU:1, one launch (start us, length us, event | category | flops | bytes accessed | tf_op | source)
XLA Modules:
  0.0 250.0 jit_solution(14751621534266897125)
XLA Ops:
  8.4 1.2 copy-done.2
  9.6 1.3 shard_map.73
  10.9 10.5 %all-to-all-start = ((bf16[32,128,128]{2,1,0:T(8,128)(2,1)}), bf16[32,128,128]{2,1,0:T(8,128)(2,1)S(1)}, u32[]{:S(2)}, u32[]{:S(2)}) async-start(bf16[32,128,128]{2,1,0:T(8,128)(2,1)} %get-tuple-element.20), calls=%async_computation | async-start | bytes 2097152 | tf_op jit(solution)/shard_map/all_to_all | solution.py:304
  22.5 3.1 %collective-permute-start = (bf16[336,128]{1,0:T(8,128)(2,1)}, bf16[336,128]{1,0:T(8,128)(2,1)S(1)}, u32[]{:S(2)}, u32[]{:S(2)}) collective-permute-start(bf16[336,128]{1,0:T(8,128)(2,1)} %get-tuple-element.41), channel_id=1, source_target_pairs={{0,64},{64,128},{128,192},{192,256},{256,320},{320,384},{384,448},... | collective-permute-start | bytes 258056 | tf_op jit(solution)/shard_map/ppermute | solution.py:285
  25.6 4.0 %collective-permute-start.1 = (bf16[336,128]{1,0:T(8,128)(2,1)}, bf16[336,128]{1,0:T(8,128)(2,1)S(1)}, u32[]{:S(2)}, u32[]{:S(2)}) collective-permute-start(bf16[336,128]{1,0:T(8,128)(2,1)} %get-tuple-element.40), channel_id=1, source_target_pairs={{0,128},{64,192},{128,256},{192,320},{256,384},{320,448},{384,0},{... | collective-permute-start | bytes 258056 | tf_op jit(solution)/shard_map/ppermute | solution.py:285
  29.6 4.3 %collective-permute-start.2 = (bf16[336,128]{1,0:T(8,128)(2,1)}, bf16[336,128]{1,0:T(8,128)(2,1)S(1)}, u32[]{:S(2)}, u32[]{:S(2)}) collective-permute-start(bf16[336,128]{1,0:T(8,128)(2,1)} %get-tuple-element.39), channel_id=1, source_target_pairs={{0,192},{64,256},{128,320},{192,384},{256,448},{320,0},{384,64},{4... | collective-permute-start | bytes 258056 | tf_op jit(solution)/shard_map/ppermute | solution.py:285
  34.0 3.9 %collective-permute-start.3 = (bf16[336,128]{1,0:T(8,128)(2,1)}, bf16[336,128]{1,0:T(8,128)(2,1)S(1)}, u32[]{:S(2)}, u32[]{:S(2)}) collective-permute-start(bf16[336,128]{1,0:T(8,128)(2,1)} %get-tuple-element.38), channel_id=1, source_target_pairs={{0,256},{64,320},{128,384},{192,448},{256,0},{320,64},{384,128},{4... | collective-permute-start | bytes 258056 | tf_op jit(solution)/shard_map/ppermute | solution.py:285
  37.9 4.4 %collective-permute-start.4 = (bf16[336,128]{1,0:T(8,128)(2,1)}, bf16[336,128]{1,0:T(8,128)(2,1)S(1)}, u32[]{:S(2)}, u32[]{:S(2)}) collective-permute-start(bf16[336,128]{1,0:T(8,128)(2,1)} %get-tuple-element.37), channel_id=1, source_target_pairs={{0,320},{64,384},{128,448},{192,0},{256,64},{320,128},{384,192},{4... | collective-permute-start | bytes 258056 | tf_op jit(solution)/shard_map/ppermute | solution.py:285
  42.3 4.6 %collective-permute-done.refs_1_ = bf16[336,128]{1,0:T(8,128)(2,1)S(1)} collective-permute-done((bf16[336,128]{1,0:T(8,128)(2,1)}, bf16[336,128]{1,0:T(8,128)(2,1)S(1)}, u32[]{:S(2)}, u32[]{:S(2)}) %collective-permute-start) | collective-permute-done | bytes 86048 | tf_op jit(solution)/shard_map/ppermute | solution.py:285
  46.9 3.8 %collective-permute-start.5 = (bf16[336,128]{1,0:T(8,128)(2,1)}, bf16[336,128]{1,0:T(8,128)(2,1)S(1)}, u32[]{:S(2)}, u32[]{:S(2)}) collective-permute-start(bf16[336,128]{1,0:T(8,128)(2,1)} %get-tuple-element.36), channel_id=1, source_target_pairs={{0,384},{64,448},{128,0},{192,64},{256,128},{320,192},{384,256},{4... | collective-permute-start | bytes 258056 | tf_op jit(solution)/shard_map/ppermute | solution.py:285
  51.6 3.8 %collective-permute-start.6 = (bf16[336,128]{1,0:T(8,128)(2,1)}, bf16[336,128]{1,0:T(8,128)(2,1)S(1)}, u32[]{:S(2)}, u32[]{:S(2)}) collective-permute-start(bf16[336,128]{1,0:T(8,128)(2,1)} %get-tuple-element.35), channel_id=1, source_target_pairs={{0,448},{64,0},{128,64},{192,128},{256,192},{320,256},{384,320},{4... | collective-permute-start | bytes 258056 | tf_op jit(solution)/shard_map/ppermute | solution.py:285
  55.5 6.1 %collective-permute-done.3.refs_4_ = bf16[336,128]{1,0:T(8,128)(2,1)S(1)} collective-permute-done((bf16[336,128]{1,0:T(8,128)(2,1)}, bf16[336,128]{1,0:T(8,128)(2,1)S(1)}, u32[]{:S(2)}, u32[]{:S(2)}) %collective-permute-start.3) | collective-permute-done | bytes 86048 | tf_op jit(solution)/shard_map/ppermute | solution.py:285
  62.5 1.3 shard_map.74
  63.9 4.5 %collective-permute-start.7 = (bf16[32,128,128]{2,1,0:T(8,128)(2,1)S(1)}, bf16[32,128,128]{2,1,0:T(8,128)(2,1)}, u32[]{:S(2)}, u32[]{:S(2)}) collective-permute-start(bf16[32,128,128]{2,1,0:T(8,128)(2,1)S(1)} %all-to-all-done.own), channel_id=1, source_target_pairs={{0,1},{1,0},{2,3},{3,2},{4,5},{5,4},{6,7},{7,6},{8,9},{9,8},{10,11... | collective-permute-start | bytes 3145736 | tf_op jit(solution)/shard_map/ppermute | solution.py:285
  69.6 1.5 shard_map.76
  71.2 13.7 %all-to-all-start.1 = ((bf16[64,104,128]{2,1,0:T(8,128)(2,1)}), bf16[64,104,128]{2,1,0:T(8,128)(2,1)}, u32[]{:S(2)}, u32[]{:S(2)}) async-start(bf16[64,104,128]{2,1,0:T(8,128)(2,1)} %shard_map.76), calls=%async_computation.2 | async-start | bytes 3407872 | tf_op jit(solution)/shard_map/all_to_all | solution.py:319
  84.9 19.1 %all-gather.4.cloned.1.call-done = bf16[9216,128]{1,0:T(8,128)(2,1)} async-done(((bf16[1152,128]{1,0:T(8,128)(2,1)}), bf16[9216,128]{1,0:T(8,128)(2,1)}) %all-gather.4.cloned.1.call-update) | async-done | bytes 2359312 | tf_op jit(solution)/shard_map/all_gather | solution.py:312
  104.1 1.7 copy-done.4
  105.7 33.2 %shard_map.75 = f32[32,168,128]{2,1,0:T(8,128)} custom-call(s32[3]{0:T(128)S(1)} %pad_add_fusion.where, f32[32,128]{1,0:T(8,128)S(1)} %broadcast_in_dim.30.wanted, bf16[32,128,128]{2,1,0:T(8,128)(2,1)S(1)} %all-to-all-done.own, bf16[32,128,128]{2,1,0:T(8,128)(2,1)} %collective-permute-done.7.other, bf16[64,144,128]{2,1,0:T(8,128)(2,1)S(1)} %bitcast.43), custom_call_target="tpu_custom_call" | custom-call | flops 17179869184 | bytes 8388608 | tf_op jit(solution)/shard_map/pallas_call | solution.py:179
  140.7 1.3 gather_fusion
  142.0 12.9 %all-to-all-start.2 = ((bf16[64,8,128]{2,1,0:T(8,128)(2,1)}), bf16[64,8,128]{2,1,0:T(8,128)(2,1)S(1)}, u32[]{:S(2)}, u32[]{:S(2)}) async-start(bf16[64,8,128]{2,1,0:T(8,128)(2,1)} %gather_fusion), calls=%async_computation.3 | async-start | bytes 262144 | tf_op jit(solution)/shard_map/all_to_all | solution.py:322
  155.0 1.5 slice.33
  156.5 1.9 gather_fusion.1
  158.4 7.0 %all-to-all-done.2 = bf16[64,8,128]{2,1,0:T(8,128)(2,1)S(1)} async-done(((bf16[64,8,128]{2,1,0:T(8,128)(2,1)}), bf16[64,8,128]{2,1,0:T(8,128)(2,1)S(1)}, u32[]{:S(2)}, u32[]{:S(2)}) %all-to-all-start.2) | async-done | bytes 131104 | tf_op jit(solution)/shard_map/all_to_all | solution.py:322
  165.3 4.9 %all-to-all-start.3 = ((bf16[64,96,128]{2,1,0:T(8,128)(2,1)}), bf16[64,96,128]{2,1,0:T(8,128)(2,1)S(1)}, u32[]{:S(2)}, u32[]{:S(2)}) async-start(bf16[64,96,128]{2,1,0:T(8,128)(2,1)} %gather_fusion.1), calls=%async_computation.4 | async-start | bytes 3145728 | tf_op jit(solution)/shard_map/all_to_all | solution.py:328
  170.4 27.4 %all-gather.1 = bf16[2304,128]{1,0:T(8,128)(2,1)S(1)} all-gather(bf16[288,128]{1,0:T(8,128)(2,1)S(1)} %pad_maximum_fusion), channel_id=3, replica_groups=mesh['y'=8,'x'=4,'z'=8,'c'=2] {'y'}, dimensions={0}, use_global_device_ids=true | all-gather | bytes 663552 | tf_op jit(solution)/shard_map/all_gather | solution.py:326
  197.8 23.4 %reduce-scatter.2.cloned.1.call-done = f32[4,168,128]{2,1,0:T(8,128)} async-done(((f32[32,168,128]{2,1,0:T(8,128)}), f32[4,168,128]{2,1,0:T(8,128)}) %reduce-scatter.2.cloned.1.call-update) | async-done | bytes 344080 | tf_op jit(solution)/shard_map/reduce_scatter | solution.py:331
  222.2 3.3 %collective-permute-start.8 = (f32[168,128]{1,0:T(8,128)S(1)}, f32[168,128]{1,0:T(8,128)S(1)}, u32[]{:S(2)}, u32[]{:S(2)}) collective-permute-start(f32[168,128]{1,0:T(8,128)S(1)} %get-tuple-element.45), channel_id=1, source_target_pairs={{0,16},{16,32},{32,48},{48,0},{1,17},{17,33},{33,49},{49,1},{2,18}... | collective-permute-start | bytes 258056 | tf_op jit(solution)/shard_map/ppermute | solution.py:285
  225.5 3.7 %collective-permute-start.9 = (f32[168,128]{1,0:T(8,128)S(1)}, f32[168,128]{1,0:T(8,128)S(1)}, u32[]{:S(2)}, u32[]{:S(2)}) collective-permute-start(f32[168,128]{1,0:T(8,128)S(1)} %get-tuple-element.44), channel_id=1, source_target_pairs={{0,32},{16,48},{32,0},{48,16},{1,33},{17,49},{33,1},{49,17},{2,34}... | collective-permute-start | bytes 258056 | tf_op jit(solution)/shard_map/ppermute | solution.py:285
  229.3 3.4 %collective-permute-start.10 = (f32[168,128]{1,0:T(8,128)S(1)}, f32[168,128]{1,0:T(8,128)S(1)}, u32[]{:S(2)}, u32[]{:S(2)}) collective-permute-start(f32[168,128]{1,0:T(8,128)S(1)} %get-tuple-element.43), channel_id=1, source_target_pairs={{0,48},{16,0},{32,16},{48,32},{1,49},{17,1},{33,17},{49,33},{2,50}... | collective-permute-start | bytes 258056 | tf_op jit(solution)/shard_map/ppermute | solution.py:285
  232.7 2.7 %collective-permute-done.10.s3 = f32[168,128]{1,0:T(8,128)S(1)} collective-permute-done((f32[168,128]{1,0:T(8,128)S(1)}, f32[168,128]{1,0:T(8,128)S(1)}, u32[]{:S(2)}, u32[]{:S(2)}) %collective-permute-start.10) | collective-permute-done | bytes 86048 | tf_op jit(solution)/shard_map/ppermute | solution.py:285
  235.4 7.8 %shard_map.77 = bf16[1536,512]{1,0:T(8,128)(2,1)} custom-call(s32[3]{0:T(128)S(1)} %pad_add_fusion.where, f32[168,128]{1,0:T(8,128)S(1)} %get-tuple-element.46.s0, f32[168,128]{1,0:T(8,128)S(1)} %collective-permute-done.8.s1, f32[168,128]{1,0:T(8,128)S(1)} %collective-permute-done.9.s2, f32[168,128]{1,0:T(8,128)S(1)} %collective-permute-done.10.s3, ...), custom_call_target="tpu_custom_call" | custom-call | tf_op jit(solution)/shard_map/pallas_call | solution.py:270
  (47 shorter events, 8.9 us)
Async XLA Ops:
  6.5 62.2 %copy-start = (s32[1,1536,32]{1,2,0:T(8,128)S(1)}, s32[1,1536,32]{1,2,0:T(8,128)}, u32[]{:S(2)}) copy-start(s32[1,1536,32]{1,2,0:T(8,128)} %param.12) | copy-start | bytes 589828
  8.4 1.2 copy-start.2
  10.9 50.7 %all-to-all-start = ((bf16[32,128,128]{2,1,0:T(8,128)(2,1)}), bf16[32,128,128]{2,1,0:T(8,128)(2,1)S(1)}, u32[]{:S(2)}, u32[]{:S(2)}) async-start(bf16[32,128,128]{2,1,0:T(8,128)(2,1)} %get-tuple-element.20), calls=%async_computation | async-start | bytes 2097152 | tf_op jit(solution)/shard_map/all_to_all | solution.py:304
  21.4 47.0 %copy-start.5 = (s32[64]{0:T(128)S(1)}, s32[64]{0:T(128)}, u32[]{:S(2)}) copy-start(s32[64]{0:T(128)} %param.10) | copy-start | bytes 772
  21.4 48.2 %copy-start.1 = (bf16[1,1536,512]{2,1,0:T(8,128)(2,1)S(1)}, bf16[1,1536,512]{2,1,0:T(8,128)(2,1)}, u32[]{:S(2)}) copy-start(bf16[1,1536,512]{2,1,0:T(8,128)(2,1)} %param.11) | copy-start | bytes 4718596
  21.4 82.6 %all-gather.4.cloned.1.call-start = ((), (), s32[]{:S(2)}) async-start(), calls=%async_computation.6 | async-start | bytes 2654208 | tf_op jit(solution)/shard_map/all_gather | solution.py:312
  22.5 24.4 %collective-permute-start = (bf16[336,128]{1,0:T(8,128)(2,1)}, bf16[336,128]{1,0:T(8,128)(2,1)S(1)}, u32[]{:S(2)}, u32[]{:S(2)}) collective-permute-start(bf16[336,128]{1,0:T(8,128)(2,1)} %get-tuple-element.41), channel_id=1, source_target_pairs={{0,64},{64,128},{128,192},{192,256},{256,320},{320,384},{384,448},... | collective-permute-start | bytes 258056 | tf_op jit(solution)/shard_map/ppermute | solution.py:285
  25.6 26.0 %collective-permute-start.1 = (bf16[336,128]{1,0:T(8,128)(2,1)}, bf16[336,128]{1,0:T(8,128)(2,1)S(1)}, u32[]{:S(2)}, u32[]{:S(2)}) collective-permute-start(bf16[336,128]{1,0:T(8,128)(2,1)} %get-tuple-element.40), channel_id=1, source_target_pairs={{0,128},{64,192},{128,256},{192,320},{256,384},{320,448},{384,0},{... | collective-permute-start | bytes 258056 | tf_op jit(solution)/shard_map/ppermute | solution.py:285
  29.6 25.9 %collective-permute-start.2 = (bf16[336,128]{1,0:T(8,128)(2,1)}, bf16[336,128]{1,0:T(8,128)(2,1)S(1)}, u32[]{:S(2)}, u32[]{:S(2)}) collective-permute-start(bf16[336,128]{1,0:T(8,128)(2,1)} %get-tuple-element.39), channel_id=1, source_target_pairs={{0,192},{64,256},{128,320},{192,384},{256,448},{320,0},{384,64},{4... | collective-permute-start | bytes 258056 | tf_op jit(solution)/shard_map/ppermute | solution.py:285
  34.0 27.6 %collective-permute-start.3 = (bf16[336,128]{1,0:T(8,128)(2,1)}, bf16[336,128]{1,0:T(8,128)(2,1)S(1)}, u32[]{:S(2)}, u32[]{:S(2)}) collective-permute-start(bf16[336,128]{1,0:T(8,128)(2,1)} %get-tuple-element.38), channel_id=1, source_target_pairs={{0,256},{64,320},{128,384},{192,448},{256,0},{320,64},{384,128},{4... | collective-permute-start | bytes 258056 | tf_op jit(solution)/shard_map/ppermute | solution.py:285
  37.9 23.7 %collective-permute-start.4 = (bf16[336,128]{1,0:T(8,128)(2,1)}, bf16[336,128]{1,0:T(8,128)(2,1)S(1)}, u32[]{:S(2)}, u32[]{:S(2)}) collective-permute-start(bf16[336,128]{1,0:T(8,128)(2,1)} %get-tuple-element.37), channel_id=1, source_target_pairs={{0,320},{64,384},{128,448},{192,0},{256,64},{320,128},{384,192},{4... | collective-permute-start | bytes 258056 | tf_op jit(solution)/shard_map/ppermute | solution.py:285
  46.9 14.7 %collective-permute-start.5 = (bf16[336,128]{1,0:T(8,128)(2,1)}, bf16[336,128]{1,0:T(8,128)(2,1)S(1)}, u32[]{:S(2)}, u32[]{:S(2)}) collective-permute-start(bf16[336,128]{1,0:T(8,128)(2,1)} %get-tuple-element.36), channel_id=1, source_target_pairs={{0,384},{64,448},{128,0},{192,64},{256,128},{320,192},{384,256},{4... | collective-permute-start | bytes 258056 | tf_op jit(solution)/shard_map/ppermute | solution.py:285
  51.6 10.0 %collective-permute-start.6 = (bf16[336,128]{1,0:T(8,128)(2,1)}, bf16[336,128]{1,0:T(8,128)(2,1)S(1)}, u32[]{:S(2)}, u32[]{:S(2)}) collective-permute-start(bf16[336,128]{1,0:T(8,128)(2,1)} %get-tuple-element.35), channel_id=1, source_target_pairs={{0,448},{64,0},{128,64},{192,128},{256,192},{320,256},{384,320},{4... | collective-permute-start | bytes 258056 | tf_op jit(solution)/shard_map/ppermute | solution.py:285
  61.6 0.9 copy-start.3
  63.9 21.1 %collective-permute-start.7 = (bf16[32,128,128]{2,1,0:T(8,128)(2,1)S(1)}, bf16[32,128,128]{2,1,0:T(8,128)(2,1)}, u32[]{:S(2)}, u32[]{:S(2)}) collective-permute-start(bf16[32,128,128]{2,1,0:T(8,128)(2,1)S(1)} %all-to-all-done.own), channel_id=1, source_target_pairs={{0,1},{1,0},{2,3},{3,2},{4,5},{5,4},{6,7},{7,6},{8,9},{9,8},{10,11... | collective-permute-start | bytes 3145736 | tf_op jit(solution)/shard_map/ppermute | solution.py:285
  71.2 68.6 %all-to-all-start.1 = ((bf16[64,104,128]{2,1,0:T(8,128)(2,1)}), bf16[64,104,128]{2,1,0:T(8,128)(2,1)}, u32[]{:S(2)}, u32[]{:S(2)}) async-start(bf16[64,104,128]{2,1,0:T(8,128)(2,1)} %shard_map.76), calls=%async_computation.2 | async-start | bytes 3407872 | tf_op jit(solution)/shard_map/all_to_all | solution.py:319
  84.9 136.3 %reduce-scatter.2.cloned.1.call-start = ((), (), s32[]{:S(2)}) async-start(), calls=%async_computation.5 | async-start | bytes 3096576 | tf_op jit(solution)/shard_map/reduce_scatter | solution.py:331
  104.1 1.7 copy-start.4
  139.0 0.7 copy-start.6
  142.0 23.3 %all-to-all-start.2 = ((bf16[64,8,128]{2,1,0:T(8,128)(2,1)}), bf16[64,8,128]{2,1,0:T(8,128)(2,1)S(1)}, u32[]{:S(2)}, u32[]{:S(2)}) async-start(bf16[64,8,128]{2,1,0:T(8,128)(2,1)} %gather_fusion), calls=%async_computation.3 | async-start | bytes 262144 | tf_op jit(solution)/shard_map/all_to_all | solution.py:322
  165.3 67.4 %all-to-all-start.3 = ((bf16[64,96,128]{2,1,0:T(8,128)(2,1)}), bf16[64,96,128]{2,1,0:T(8,128)(2,1)S(1)}, u32[]{:S(2)}, u32[]{:S(2)}) async-start(bf16[64,96,128]{2,1,0:T(8,128)(2,1)} %gather_fusion.1), calls=%async_computation.4 | async-start | bytes 3145728 | tf_op jit(solution)/shard_map/all_to_all | solution.py:328
  222.2 10.5 %collective-permute-start.8 = (f32[168,128]{1,0:T(8,128)S(1)}, f32[168,128]{1,0:T(8,128)S(1)}, u32[]{:S(2)}, u32[]{:S(2)}) collective-permute-start(f32[168,128]{1,0:T(8,128)S(1)} %get-tuple-element.45), channel_id=1, source_target_pairs={{0,16},{16,32},{32,48},{48,0},{1,17},{17,33},{33,49},{49,1},{2,18}... | collective-permute-start | bytes 258056 | tf_op jit(solution)/shard_map/ppermute | solution.py:285
  225.5 7.2 %collective-permute-start.9 = (f32[168,128]{1,0:T(8,128)S(1)}, f32[168,128]{1,0:T(8,128)S(1)}, u32[]{:S(2)}, u32[]{:S(2)}) collective-permute-start(f32[168,128]{1,0:T(8,128)S(1)} %get-tuple-element.44), channel_id=1, source_target_pairs={{0,32},{16,48},{32,0},{48,16},{1,33},{17,49},{33,1},{49,17},{2,34}... | collective-permute-start | bytes 258056 | tf_op jit(solution)/shard_map/ppermute | solution.py:285
  229.3 6.1 %collective-permute-start.10 = (f32[168,128]{1,0:T(8,128)S(1)}, f32[168,128]{1,0:T(8,128)S(1)}, u32[]{:S(2)}, u32[]{:S(2)}) collective-permute-start(f32[168,128]{1,0:T(8,128)S(1)} %get-tuple-element.43), channel_id=1, source_target_pairs={{0,48},{16,0},{32,16},{48,32},{1,49},{17,1},{33,17},{49,33},{2,50}... | collective-permute-start | bytes 258056 | tf_op jit(solution)/shard_map/ppermute | solution.py:285
Sparse Core Ops, SparseCore 0:
  64.0 39.9 all-gather.3
  139.1 82.0 reduce-scatter.1

commit v3 on v2

--- a/solution.py
+++ b/solution.py
@@ -21,30 +21,7 @@
 SMEM = pl.BlockSpec(memory_space=pltpu.SMEM)
 
 
-def sort_kernel(where, *refs):
-    came, (panels, rows) = refs[:NY], refs[NY:]
-    for s in range(NY):
-        panels[s * 144 : (s + 1) * 144, :] = came[s][0:144, :]
-
-        @pl.when(where[2] == s)
-        def _(s=s):
-            rows[...] = came[s][144:336, :].astype(f32)
-
-
-def sort(where, came):
-    return pl.pallas_call(
-        sort_kernel,
-        out_shape=(
-            jax.ShapeDtypeStruct((NY * 144, 128), bf16),
-            jax.ShapeDtypeStruct((192, 128), f32),
-        ),
-        in_specs=[SMEM] + [VMEM] * NY,
-        out_specs=(VMEM,) * 2,
-        compiler_params=pltpu.CompilerParams(vmem_limit_bytes=16 * 1024 * 1024),
-    )(where, *came)
-
-
-def pack_kernel(weights, patterns, inverse, rows, pieces):
+def pack_kernel(weights, patterns, inverse, pieces):
     numbers = patterns[...].astype(f32)
     rest = inverse[...]
     parts = []
@@ -60,53 +37,64 @@
         k, q = p // 16, p % 16
         pieces[p, 0:96, :] = weights[96 * q : 96 * (q + 1), 128 * k : 128 * (k + 1)]
         pieces[p, 96:104, :] = jnp.concatenate(
-            [extra[2 * p : 2 * p + 2], rows[3 * p : 3 * p + 3, :], jnp.zeros((3, 128), f32)], axis=0
+            [extra[2 * p : 2 * p + 2], jnp.zeros((6, 128), f32)], axis=0
         ).astype(bf16)
 
 
-def pack(weights, patterns, inverse, rows):
+def pack(weights, patterns, inverse):
     return pl.pallas_call(
         pack_kernel,
         out_shape=jax.ShapeDtypeStruct((64, 104, 128), bf16),
-        in_specs=[VMEM] * 4,
+        in_specs=[VMEM] * 3,
         out_specs=VMEM,
         compiler_params=pltpu.CompilerParams(vmem_limit_bytes=16 * 1024 * 1024),
-    )(weights, patterns, inverse, rows)
-
-
-def prep_kernel(tokens, routes, rows, blocks, notes):
+    )(weights, patterns, inverse)
+
+
+def join_kernel(*refs):
+    for s in range(NY):
+        refs[NY][s * 144 : (s + 1) * 144, :] = refs[s][...]
+
+
+def join(came):
+    return pl.pallas_call(
+        join_kernel,
+        out_shape=jax.ShapeDtypeStruct((NY * 144, 128), bf16),
+        in_specs=[VMEM] * NY,
+        out_specs=VMEM,
+        compiler_params=pltpu.CompilerParams(vmem_limit_bytes=16 * 1024 * 1024),
+    )(*came)
+
+
+def prep_kernel(tokens, routes, blocks, panel):
     squares = jnp.zeros((128, 128), f32)
     for s in range(32):
         part = tokens[:, s * 128 : (s + 1) * 128]
         blocks[s] = part
         wide = part.astype(f32)
         squares = squares + wide * wide
-    turned = tokens[:, 0:128].astype(f32).T.astype(bf16)
+    panel[0:128, :] = tokens[:, 0:128].astype(f32).T.astype(bf16)
     norms = jnp.sum(squares.T, axis=0, keepdims=True) * (1.0 / D)
     high = norms.astype(bf16).astype(f32)
     named = jnp.concatenate(
         [routes[...].astype(f32), jnp.zeros((128, 120), f32)], axis=1
     ).T
-    facts = jnp.concatenate(
+    panel[128:144, :] = jnp.concatenate(
         [named[0:8], high, norms - high, jnp.zeros((6, 128), f32)], axis=0
     ).astype(bf16)
-    for s in range(NY):
-        notes[s, 0:128, :] = turned
-        notes[s, 128:144, :] = facts
-        notes[s, 144:336, :] = rows[s * 192 : (s + 1) * 192, :]
-
-
-def prepare(tokens, routes, rows):
+
+
+def prepare(tokens, routes):
     return pl.pallas_call(
         prep_kernel,
         out_shape=(
             jax.ShapeDtypeStruct((32, 128, 128), bf16),
-            jax.ShapeDtypeStruct((NY, 336, 128), bf16),
+            jax.ShapeDtypeStruct((144, 128), bf16),
         ),
-        in_specs=[VMEM] * 3,
+        in_specs=[VMEM] * 2,
         out_specs=(VMEM,) * 2,
         compiler_params=pltpu.CompilerParams(vmem_limit_bytes=16 * 1024 * 1024),
-    )(tokens, routes, rows)
+    )(tokens, routes)
 
 
 def gram_kernel(where, wanted, own, other, panels, out, left_all, right, squares, marks, left, total, norms):
@@ -206,16 +194,16 @@
     return found
 
 
-def refit_kernel(where, s0, s1, s2, s3, shared, held, out, normed, scaled, inverse):
-    x, y = where[0], where[2]
-    scaling = s0[161:162, :] + EPSILON
+def refit_kernel(where, total, shared, held, out, normed, scaled, inverse):
+    y = where[2]
+    scaling = total[0, 161:162, :] + EPSILON
     a = lax.broadcasted_iota(jnp.int32, (128, 128), 0)
     b = lax.broadcasted_iota(jnp.int32, (128, 128), 1)
-    for step, sums in enumerate((s0, s1, s2, s3)):
-        q = lax.rem(x - step + NX, NX)
+    for q in range(NX):
+        sums = total[q]
         diagonal = sums[160:161, :] / scaling + DAMPING
         high, low = parts_of(sums[0:128, :] / scaling / diagonal, 2)
-        at = pl.ds(pl.multiple_of(q * 128, 128), 128)
+        at = slice(q * 128, (q + 1) * 128)
         scaled[0:128, at] = high
         scaled[128:256, at] = low
         scaled[256:384, at] = high
@@ -223,7 +211,7 @@
         lanes = lax.broadcasted_iota(jnp.int32, (32, 128), 1)
         damped = sums[128:160, :] / scaling + jnp.where(rows == lanes, DAMPING, 0.0)
         for k, part in enumerate(parts_of(damped, 3)):
-            normed[pl.ds(pl.multiple_of(k * 128 + q * 32, 32), 32), :] = part
+            normed[k * 128 + q * 32 : k * 128 + q * 32 + 32, :] = part
     for q in range(NY):
         part = [shared[q, 240 + 16 * k : 256 + 16 * k, :] for k in range(3)]
         for k, source in enumerate((0, 1, 0, 2, 1, 0)):
@@ -257,7 +245,7 @@
         )
         for k in range(4):
             for half in range(2):
-                piece = held[16 * k + 2 * q + half, :, :].astype(f32)
+                piece = held[16 * k + 2 * q + half, 0:96, :].astype(f32)
                 fixed = piece - correction[half * 96 : (half + 1) * 96, k * 128 : (k + 1) * 128]
                 out[pl.ds(pl.multiple_of(q * 192 + half * 96, 32), 96), k * 128 : (k + 1) * 128] = fixed.astype(bf16)
 
@@ -270,7 +258,7 @@
     return pl.pallas_call(
         refit_kernel,
         out_shape=jax.ShapeDtypeStruct((FF, 512), bf16),
-        in_specs=[SMEM] + [VMEM] * 6,
+        in_specs=[SMEM] + [VMEM] * 3,
         out_specs=VMEM,
         scratch_shapes=[
             pltpu.VMEM((384, 128), bf16),
@@ -278,7 +266,7 @@
             pltpu.VMEM((768, 128), bf16),
         ],
         compiler_params=pltpu.CompilerParams(vmem_limit_bytes=32 * 1024 * 1024),
-    )(where, *sums, shared, held)
+    )(where, sums, shared, held)
 
 
 def swap(value, axis, size, step):
@@ -300,41 +288,28 @@
         lax.dynamic_index_in_dim(order, c, 0, keepdims=False)[:, None], (HELD, 128)
     ).astype(f32)
 
-    blocks, notes = prepare(tokens, routes, weights[0, :, 0:PANEL])
-    own = lax.all_to_all(blocks, ("y", "x"), 0, 0, tiled=True)
-
-    def note(step):
-        return lax.dynamic_index_in_dim(notes, (y + step) % NY, 0, keepdims=False)
-
-    came = [note(0)] + [swap(note(step), "y", NY, step) for step in range(1, NY)]
-    own, *came = lax.optimization_barrier((own, *came))
-    panels, rows = sort(where, came)
-    panels = lax.all_gather(panels, ("x", "c"), axis=0, tiled=False).reshape(64, 144, 128)
     pieces = pack(
         weights[0],
         lax.dynamic_slice_in_dim(patterns[0], y * 192, 192, 0),
         lax.dynamic_slice_in_dim(inverse[0], y * 16, 16, 0),
-        rows,
     )
     spread = lax.all_to_all(pieces, EXPERT, 0, 0, tiled=True)
+    blocks, panel = prepare(tokens, routes)
+    came = [panel] + [swap(panel, "y", NY, step) for step in range(1, NY)]
+    spread, *came = lax.optimization_barrier((spread, *came))
+    panels = lax.all_gather(join(came), ("x", "c"), axis=0, tiled=False).reshape(64, 144, 128)
+    own = lax.all_to_all(after(blocks, spread), ("y", "x"), 0, 0, tiled=True)
     other = swap(own, "c", NC, 1)
-    tails = jnp.take(spread[:, 96:104], source, axis=0, mode="clip")
-    tails = lax.all_to_all(tails, EXPERT, 0, 0, tiled=True)
-    shared = jnp.concatenate(
-        [tails[:, 2:5].reshape(192, 128), tails[:, 0:2].reshape(128, 128)[0:96]], axis=0
-    )
+    spread = jnp.take(spread, source, axis=0, mode="clip")
+    held = lax.all_to_all(after(spread, own), EXPERT, 0, 0, tiled=True)
+
+    sums = gram(where, wanted, own, other, panels)
+    sums = lax.psum_scatter(after(sums, held), "z", scatter_dimension=0, tiled=True)
+    moved = held[0:16, 0:96].reshape(NY, 192, 128)
+    moved = lax.all_to_all(moved, "y", 0, 0, tiled=True)[0]
+    shared = jnp.concatenate([moved, held[:, 96:98].reshape(128, 128)[0:96]], axis=0)
     shared = lax.all_gather(shared, "y", axis=0, tiled=False)
-    held = jnp.take(spread[:, 0:96], source, axis=0, mode="clip")
-    held = lax.all_to_all(after(held, tails), EXPERT, 0, 0, tiled=True)
-
-    sums = gram(where, wanted, own, other, panels)
-    sums = lax.psum_scatter(sums, "z", scatter_dimension=0, tiled=True)
-    sums = after(sums, shared)
-
-    def column(step):
-        return lax.dynamic_index_in_dim(sums, (x + step) % NX, 0, keepdims=False)
-
-    sums = [column(0)] + [swap(column(step), "x", NX, step) for step in range(1, NX)]
+    sums = lax.all_to_all(after(sums, shared), "x", 0, 0, tiled=True)
     return refit(where, sums, shared, held)[None]
 
 

time: 254 us -> 226 us (0.89)
  starting transfers between devices: 84.4 us -> 66.4 us
  waiting for transfers between devices: 63.7 us -> 55.6 us
  local copies, waits for them, and re-layouts: 15.2 us -> 10.2 us
  blocking collectives: 27.4 us -> 31.2 us
    all_to_all x3, waiting for transfers between devices: 6.96 us -> 41.1 us  [the longest x1 23.2 us: shards(): own = lax.all_to_all(after(blocks, spread), ('y', 'x'), 0, 0, tiled=True)]
    reduce_scatter x1, waiting for transfers between devices: 23.4 us -> 0.01 us  [shards(): lax.psum_scatter(after(sums, held), 'z', scatter_dimension=0, tiled=True)]
    all_gather x1, waiting for transfers between devices: 19.1 us -> 0.01 us  [shards(): lax.all_gather(join(came), ('x', 'c'), axis=0, tiled=False)]
    ppermute x11 -> x8, starting transfers between devices: 42.4 us -> 30.9 us  [swap(): lax.ppermute(value, axis, [(i, (i + step) % size) for i in range(size)])]
    all_to_all x1, waiting for transfers between devices: 0.01 us -> 10.5 us  [shards(): spread = lax.all_to_all(pieces, EXPERT, 0, 0, tiled=True)]
    ppermute x11 -> x8, waiting for transfers between devices: 14.3 us -> 3.97 us  [swap(): lax.ppermute(value, axis, [(i, (i + step) % size) for i in range(size)])]
    all_to_all x0 -> x1, blocking collectives: none -> 9.39 us  [shards(): sums = lax.all_to_all(after(sums, shared), 'x', 0, 0, tiled=True)]
    all_to_all x3, starting transfers between devices: 28.3 us -> 20.5 us  [the longest x1 9.76 us: shards(): own = lax.all_to_all(after(blocks, spread), ('y', 'x'), 0, 0, tiled=True)]
  transfers between devices with their start and end apart: 17 -> 14, of which waited for: 7 -> 6; matrix products, arithmetic and copies ran while one was open for 4% -> 2% of each run, Pallas kernels for 14% -> 16%
where the time goes in v3:
time: 226 us; the launch traced here: 222 us
  starting transfers between devices  66.4 us (29%)
  waiting for transfers between devices  55.6 us (25%)
  Pallas kernels  44.5 us (20%)
  blocking collectives  31.2 us (14%)
  between operations  13.6 us (6%)
  local copies, waits for them, and re-layouts  10.2 us (5%)
    pallas_call x1, Pallas kernels, gram(): pl.pallas_call(gram_kernel, out_shape=jax.ShapeDtypeStruct((HELD, ROWS, 1...  33.2 us
    ppermute x8, starting transfers between devices, swap(): lax.ppermute(value, axis, [(i, (i + step) % size) for i in range(size)])  30.9 us
    all_to_all x1, waiting for transfers between devices, shards(): own = lax.all_to_all(after(blocks, spread), ('y', 'x'), 0, 0, tiled=True)  23.2 us
    all_gather x1, blocking collectives, shards(): shared = lax.all_gather(shared, 'y', axis=0, tiled=False)  21.8 us
    all_to_all x1, waiting for transfers between devices, shards(): moved = lax.all_to_all(moved, 'y', 0, 0, tiled=True)[0]  15.1 us
    all_to_all x1, starting transfers between devices, shards(): spread = lax.all_to_all(pieces, EXPERT, 0, 0, tiled=True)  15 us
    all_to_all x1, waiting for transfers between devices, shards(): spread = lax.all_to_all(pieces, EXPERT, 0, 0, tiled=True)  10.5 us
    all_to_all x1, starting transfers between devices, shards(): own = lax.all_to_all(after(blocks, spread), ('y', 'x'), 0, 0, tiled=True)  9.76 us
  transfers between devices with their start and end apart: 14, of which 6 were waited for; matrix products, arithmetic and copies ran while one was open for 2% of the time, Pallas kernels for 16%

profile of v3, /device:TPU:1, one launch (start us, length us, event | category | flops | bytes accessed | tf_op | source)
XLA Modules:
  0.0 221.9 jit_solution(4291302256257150547)
XLA Ops:
  6.5 0.9 copy-done
  7.6 0.7 dynamic-slice_bitcast_fusion.inverse
  8.3 1.4 copy-done.1
  9.8 1.5 shard_map.74
  11.3 15.0 %all-to-all-start = ((bf16[64,104,128]{2,1,0:T(8,128)(2,1)}), bf16[64,104,128]{2,1,0:T(8,128)(2,1)S(1)}, u32[]{:S(2)}, u32[]{:S(2)}) async-start(bf16[64,104,128]{2,1,0:T(8,128)(2,1)} %shard_map.74), calls=%async_computation | async-start | bytes 3407872 | tf_op jit(solution)/shard_map/all_to_all | solution.py:296
  26.4 1.3 shard_map.73
  27.7 3.3 %collective-permute-start = (bf16[144,128]{1,0:T(8,128)(2,1)S(1)}, bf16[144,128]{1,0:T(8,128)(2,1)S(1)}, u32[]{:S(2)}, u32[]{:S(2)}) collective-permute-start(bf16[144,128]{1,0:T(8,128)(2,1)S(1)} %get-tuple-element.24.refs_0_), channel_id=1, source_target_pairs={{0,64},{64,128},{128,192},{192,256},{256,320},{320,384},{384,448},... | collective-permute-start | bytes 110600 | tf_op jit(solution)/shard_map/ppermute | solution.py:273
  31.1 4.2 %collective-permute-start.1 = (bf16[144,128]{1,0:T(8,128)(2,1)S(1)}, bf16[144,128]{1,0:T(8,128)(2,1)S(1)}, u32[]{:S(2)}, u32[]{:S(2)}) collective-permute-start(bf16[144,128]{1,0:T(8,128)(2,1)S(1)} %get-tuple-element.24.refs_0_), channel_id=1, source_target_pairs={{0,128},{64,192},{128,256},{192,320},{256,384},{320,448},{384,0},{... | collective-permute-start | bytes 110600 | tf_op jit(solution)/shard_map/ppermute | solution.py:273
  35.3 4.6 %collective-permute-start.2 = (bf16[144,128]{1,0:T(8,128)(2,1)S(1)}, bf16[144,128]{1,0:T(8,128)(2,1)S(1)}, u32[]{:S(2)}, u32[]{:S(2)}) collective-permute-start(bf16[144,128]{1,0:T(8,128)(2,1)S(1)} %get-tuple-element.24.refs_0_), channel_id=1, source_target_pairs={{0,192},{64,256},{128,320},{192,384},{256,448},{320,0},{384,64},{4... | collective-permute-start | bytes 110600 | tf_op jit(solution)/shard_map/ppermute | solution.py:273
  39.9 3.5 %collective-permute-start.3 = (bf16[144,128]{1,0:T(8,128)(2,1)S(1)}, bf16[144,128]{1,0:T(8,128)(2,1)S(1)}, u32[]{:S(2)}, u32[]{:S(2)}) collective-permute-start(bf16[144,128]{1,0:T(8,128)(2,1)S(1)} %get-tuple-element.24.refs_0_), channel_id=1, source_target_pairs={{0,256},{64,320},{128,384},{192,448},{256,0},{320,64},{384,128},{4... | collective-permute-start | bytes 110600 | tf_op jit(solution)/shard_map/ppermute | solution.py:273
  43.5 4.9 %collective-permute-start.4 = (bf16[144,128]{1,0:T(8,128)(2,1)S(1)}, bf16[144,128]{1,0:T(8,128)(2,1)S(1)}, u32[]{:S(2)}, u32[]{:S(2)}) collective-permute-start(bf16[144,128]{1,0:T(8,128)(2,1)S(1)} %get-tuple-element.24.refs_0_), channel_id=1, source_target_pairs={{0,320},{64,384},{128,448},{192,0},{256,64},{320,128},{384,192},{4... | collective-permute-start | bytes 110600 | tf_op jit(solution)/shard_map/ppermute | solution.py:273
  48.4 5.0 %collective-permute-start.5 = (bf16[144,128]{1,0:T(8,128)(2,1)S(1)}, bf16[144,128]{1,0:T(8,128)(2,1)S(1)}, u32[]{:S(2)}, u32[]{:S(2)}) collective-permute-start(bf16[144,128]{1,0:T(8,128)(2,1)S(1)} %get-tuple-element.24.refs_0_), channel_id=1, source_target_pairs={{0,384},{64,448},{128,0},{192,64},{256,128},{320,192},{384,256},{4... | collective-permute-start | bytes 110600 | tf_op jit(solution)/shard_map/ppermute | solution.py:273
  53.4 3.0 %collective-permute-start.6 = (bf16[144,128]{1,0:T(8,128)(2,1)S(1)}, bf16[144,128]{1,0:T(8,128)(2,1)S(1)}, u32[]{:S(2)}, u32[]{:S(2)}) collective-permute-start(bf16[144,128]{1,0:T(8,128)(2,1)S(1)} %get-tuple-element.24.refs_0_), channel_id=1, source_target_pairs={{0,448},{64,0},{128,64},{192,128},{256,192},{320,256},{384,320},{4... | collective-permute-start | bytes 110600 | tf_op jit(solution)/shard_map/ppermute | solution.py:273
  56.4 2.0 collective-permute-done.6.refs_7_
  58.4 10.5 %all-to-all-done = bf16[64,104,128]{2,1,0:T(8,128)(2,1)S(1)} async-done(((bf16[64,104,128]{2,1,0:T(8,128)(2,1)}), bf16[64,104,128]{2,1,0:T(8,128)(2,1)S(1)}, u32[]{:S(2)}, u32[]{:S(2)}) %all-to-all-start) | async-done | bytes 1703968 | tf_op jit(solution)/shard_map/all_to_all | solution.py:296
  68.9 0.8 shard_map.75
  69.7 0.6 copy-done.4
  70.2 9.8 %all-to-all-start.1 = ((bf16[32,128,128]{2,1,0:T(8,128)(2,1)}), bf16[32,128,128]{2,1,0:T(8,128)(2,1)S(1)}, u32[]{:S(2)}, u32[]{:S(2)}) async-start(bf16[32,128,128]{2,1,0:T(8,128)(2,1)} %get-tuple-element.23), calls=%async_computation.1 | async-start | bytes 2097152 | tf_op jit(solution)/shard_map/all_to_all | solution.py:301
  80.2 3.5 %gather_fusion = bf16[64,104,128]{2,1,0:T(8,128)(2,1)} fusion(bf16[64,104,128]{2,1,0:T(8,128)(2,1)} %copy-done.4, s32[1024]{0:T(1024)S(1)} %pad_clamp_fusion), kind=kCustom, calls=%fused_computation | custom fusion | bytes 3408128 | tf_op jit(solution)/shard_map/jit(_take)/gather | solution.py:303
  83.7 23.2 %all-to-all-done.1.own = bf16[32,128,128]{2,1,0:T(8,128)(2,1)S(1)} async-done(((bf16[32,128,128]{2,1,0:T(8,128)(2,1)}), bf16[32,128,128]{2,1,0:T(8,128)(2,1)S(1)}, u32[]{:S(2)}, u32[]{:S(2)}) %all-to-all-start.1) | async-done | bytes 1048608 | tf_op jit(solution)/shard_map/all_to_all | solution.py:301
  106.9 7.3 %all-to-all-start.2 = ((bf16[64,104,128]{2,1,0:T(8,128)(2,1)}), bf16[64,104,128]{2,1,0:T(8,128)(2,1)S(1)}, u32[]{:S(2)}, u32[]{:S(2)}) async-start(bf16[64,104,128]{2,1,0:T(8,128)(2,1)} %gather_fusion), calls=%async_computation.2 | async-start | bytes 3407872 | tf_op jit(solution)/shard_map/all_to_all | solution.py:304
  114.2 2.4 %collective-permute-start.7 = (bf16[32,128,128]{2,1,0:T(8,128)(2,1)S(1)}, bf16[32,128,128]{2,1,0:T(8,128)(2,1)}, u32[]{:S(2)}, u32[]{:S(2)}) collective-permute-start(bf16[32,128,128]{2,1,0:T(8,128)(2,1)S(1)} %all-to-all-done.1.own), channel_id=1, source_target_pairs={{0,1},{1,0},{2,3},{3,2},{4,5},{5,4},{6,7},{7,6},{8,9},{9,8},{10,11... | collective-permute-start | bytes 3145736 | tf_op jit(solution)/shard_map/ppermute | solution.py:273
  117.0 2.0 collective-permute-done.7.other
  119.1 1.7 copy-done.3
  120.7 33.2 %shard_map.76 = f32[32,168,128]{2,1,0:T(8,128)} custom-call(s32[3]{0:T(128)S(1)} %pad_add_fusion.where, f32[32,128]{1,0:T(8,128)S(1)} %broadcast_in_dim.28.wanted, bf16[32,128,128]{2,1,0:T(8,128)(2,1)S(1)} %all-to-all-done.1.own, bf16[32,128,128]{2,1,0:T(8,128)(2,1)} %collective-permute-done.7.other, bf16[64,144,128]{2,1,0:T(8,128)(2,1)S(1)} %bitcast.20), custom_call_target="tpu_custom_call" | custom-call | flops 17179869184 | bytes 8388608 | tf_op jit(solution)/shard_map/pallas_call | solution.py:167
  154.0 2.8 %all-to-all-done.2.held = bf16[64,104,128]{2,1,0:T(8,128)(2,1)S(1)} async-done(((bf16[64,104,128]{2,1,0:T(8,128)(2,1)}), bf16[64,104,128]{2,1,0:T(8,128)(2,1)S(1)}, u32[]{:S(2)}, u32[]{:S(2)}) %all-to-all-start.2) | async-done | bytes 1703968 | tf_op jit(solution)/shard_map/all_to_all | solution.py:304
  156.8 0.8 slice.20
  157.6 3.5 %all-to-all-start.3 = ((bf16[8,192,128]{2,1,0:T(8,128)(2,1)}), bf16[8,192,128]{2,1,0:T(8,128)(2,1)S(1)}, u32[]{:S(2)}, u32[]{:S(2)}) async-start(bf16[8,192,128]{2,1,0:T(8,128)(2,1)} %bitcast.9), calls=%async_computation.4 | async-start | bytes 786432 | tf_op jit(solution)/shard_map/all_to_all | solution.py:309
  161.1 15.1 %all-to-all-done.3 = bf16[8,192,128]{2,1,0:T(8,128)(2,1)S(1)} async-done(((bf16[8,192,128]{2,1,0:T(8,128)(2,1)}), bf16[8,192,128]{2,1,0:T(8,128)(2,1)S(1)}, u32[]{:S(2)}, u32[]{:S(2)}) %all-to-all-start.3) | async-done | bytes 393248 | tf_op jit(solution)/shard_map/all_to_all | solution.py:309
  176.2 21.8 %all-gather.1 = bf16[2304,128]{1,0:T(8,128)(2,1)S(1)} all-gather(bf16[288,128]{1,0:T(8,128)(2,1)S(1)} %pad_maximum_fusion), channel_id=3, replica_groups=mesh['y'=8,'x'=4,'z'=8,'c'=2] {'y'}, dimensions={0}, use_global_device_ids=true | all-gather | bytes 663552 | tf_op jit(solution)/shard_map/all_gather | solution.py:311
  198.0 9.4 %all_to_all.25.total = f32[4,168,128]{2,1,0:T(8,128)S(1)} all-to-all(f32[4,168,128]{2,1,0:T(8,128)} %reduce-scatter.2.cloned.1.call-done), channel_id=1, replica_groups=mesh['y'=8,'x'=4,'z'=8,'c'=2] {'x'}, dimensions={0} | all-to-all | bytes 688128 | tf_op jit(solution)/shard_map/all_to_all | solution.py:312
  207.3 7.7 %shard_map.77 = bf16[1536,512]{1,0:T(8,128)(2,1)} custom-call(s32[3]{0:T(128)S(1)} %pad_add_fusion.where, f32[4,168,128]{2,1,0:T(8,128)S(1)} %all_to_all.25.total, bf16[8,288,128]{2,1,0:T(8,128)(2,1)S(1)} %bitcast.17, bf16[64,104,128]{2,1,0:T(8,128)(2,1)S(1)} %all-to-all-done.2.held), custom_call_target="tpu_custom_call" | custom-call | tf_op jit(solution)/shard_map/pallas_call | solution.py:258
  (38 shorter events, 1.1 us)
Async XLA Ops:
  6.5 0.9 copy-start
  8.3 1.4 copy-start.1
  11.3 15.0 %copy-start.5 = (s32[128,8]{0,1:T(8,128)S(1)}, s32[128,8]{0,1:T(8,128)}, u32[]{:S(2)}) copy-start(s32[128,8]{0,1:T(8,128)} %param.8) | copy-start | bytes 12292
  11.3 15.1 %copy-start.2 = (bf16[128,4096]{1,0:T(8,128)(2,1)S(1)}, bf16[128,4096]{1,0:T(8,128)(2,1)}, u32[]{:S(2)}) copy-start(bf16[128,4096]{1,0:T(8,128)(2,1)} %tokens.1) | copy-start | bytes 3145732
  11.3 57.6 %all-to-all-start = ((bf16[64,104,128]{2,1,0:T(8,128)(2,1)}), bf16[64,104,128]{2,1,0:T(8,128)(2,1)S(1)}, u32[]{:S(2)}, u32[]{:S(2)}) async-start(bf16[64,104,128]{2,1,0:T(8,128)(2,1)} %shard_map.74), calls=%async_computation | async-start | bytes 3407872 | tf_op jit(solution)/shard_map/all_to_all | solution.py:296
  26.3 92.7 %all-gather.4.cloned.1.call-start = ((), (), s32[]{:S(2)}) async-start(), calls=%async_computation.7 | async-start | bytes 2654208 | tf_op jit(solution)/shard_map/all_gather | solution.py:300
  27.7 52.3 %copy-start.6 = (s32[64]{0:T(128)S(1)}, s32[64]{0:T(128)}, u32[]{:S(2)}) copy-start(s32[64]{0:T(128)} %param.10) | copy-start | bytes 772
  27.7 52.3 %copy-start.7 = (s32[64]{0:T(128)S(1)}, s32[64]{0:T(128)}, u32[]{:S(2)}) copy-start(s32[64]{0:T(128)} %param.9) | copy-start | bytes 772
  27.7 20.6 %collective-permute-start = (bf16[144,128]{1,0:T(8,128)(2,1)S(1)}, bf16[144,128]{1,0:T(8,128)(2,1)S(1)}, u32[]{:S(2)}, u32[]{:S(2)}) collective-permute-start(bf16[144,128]{1,0:T(8,128)(2,1)S(1)} %get-tuple-element.24.refs_0_), channel_id=1, source_target_pairs={{0,64},{64,128},{128,192},{192,256},{256,320},{320,384},{384,448},... | collective-permute-start | bytes 110600 | tf_op jit(solution)/shard_map/ppermute | solution.py:273
  31.1 22.3 %collective-permute-start.1 = (bf16[144,128]{1,0:T(8,128)(2,1)S(1)}, bf16[144,128]{1,0:T(8,128)(2,1)S(1)}, u32[]{:S(2)}, u32[]{:S(2)}) collective-permute-start(bf16[144,128]{1,0:T(8,128)(2,1)S(1)} %get-tuple-element.24.refs_0_), channel_id=1, source_target_pairs={{0,128},{64,192},{128,256},{192,320},{256,384},{320,448},{384,0},{... | collective-permute-start | bytes 110600 | tf_op jit(solution)/shard_map/ppermute | solution.py:273
  35.3 21.1 %collective-permute-start.2 = (bf16[144,128]{1,0:T(8,128)(2,1)S(1)}, bf16[144,128]{1,0:T(8,128)(2,1)S(1)}, u32[]{:S(2)}, u32[]{:S(2)}) collective-permute-start(bf16[144,128]{1,0:T(8,128)(2,1)S(1)} %get-tuple-element.24.refs_0_), channel_id=1, source_target_pairs={{0,192},{64,256},{128,320},{192,384},{256,448},{320,0},{384,64},{4... | collective-permute-start | bytes 110600 | tf_op jit(solution)/shard_map/ppermute | solution.py:273
  39.9 16.4 %collective-permute-start.3 = (bf16[144,128]{1,0:T(8,128)(2,1)S(1)}, bf16[144,128]{1,0:T(8,128)(2,1)S(1)}, u32[]{:S(2)}, u32[]{:S(2)}) collective-permute-start(bf16[144,128]{1,0:T(8,128)(2,1)S(1)} %get-tuple-element.24.refs_0_), channel_id=1, source_target_pairs={{0,256},{64,320},{128,384},{192,448},{256,0},{320,64},{384,128},{4... | collective-permute-start | bytes 110600 | tf_op jit(solution)/shard_map/ppermute | solution.py:273
  43.5 12.9 %collective-permute-start.4 = (bf16[144,128]{1,0:T(8,128)(2,1)S(1)}, bf16[144,128]{1,0:T(8,128)(2,1)S(1)}, u32[]{:S(2)}, u32[]{:S(2)}) collective-permute-start(bf16[144,128]{1,0:T(8,128)(2,1)S(1)} %get-tuple-element.24.refs_0_), channel_id=1, source_target_pairs={{0,320},{64,384},{128,448},{192,0},{256,64},{320,128},{384,192},{4... | collective-permute-start | bytes 110600 | tf_op jit(solution)/shard_map/ppermute | solution.py:273
  48.4 8.0 %collective-permute-start.5 = (bf16[144,128]{1,0:T(8,128)(2,1)S(1)}, bf16[144,128]{1,0:T(8,128)(2,1)S(1)}, u32[]{:S(2)}, u32[]{:S(2)}) collective-permute-start(bf16[144,128]{1,0:T(8,128)(2,1)S(1)} %get-tuple-element.24.refs_0_), channel_id=1, source_target_pairs={{0,384},{64,448},{128,0},{192,64},{256,128},{320,192},{384,256},{4... | collective-permute-start | bytes 110600 | tf_op jit(solution)/shard_map/ppermute | solution.py:273
  53.4 5.0 %collective-permute-start.6 = (bf16[144,128]{1,0:T(8,128)(2,1)S(1)}, bf16[144,128]{1,0:T(8,128)(2,1)S(1)}, u32[]{:S(2)}, u32[]{:S(2)}) collective-permute-start(bf16[144,128]{1,0:T(8,128)(2,1)S(1)} %get-tuple-element.24.refs_0_), channel_id=1, source_target_pairs={{0,448},{64,0},{128,64},{192,128},{256,192},{320,256},{384,320},{4... | collective-permute-start | bytes 110600 | tf_op jit(solution)/shard_map/ppermute | solution.py:273
  68.9 1.4 copy-start.4
  70.2 36.7 %all-to-all-start.1 = ((bf16[32,128,128]{2,1,0:T(8,128)(2,1)}), bf16[32,128,128]{2,1,0:T(8,128)(2,1)S(1)}, u32[]{:S(2)}, u32[]{:S(2)}) async-start(bf16[32,128,128]{2,1,0:T(8,128)(2,1)} %get-tuple-element.23), calls=%async_computation.1 | async-start | bytes 2097152 | tf_op jit(solution)/shard_map/all_to_all | solution.py:301
  106.9 49.9 %all-to-all-start.2 = ((bf16[64,104,128]{2,1,0:T(8,128)(2,1)}), bf16[64,104,128]{2,1,0:T(8,128)(2,1)S(1)}, u32[]{:S(2)}, u32[]{:S(2)}) async-start(bf16[64,104,128]{2,1,0:T(8,128)(2,1)} %gather_fusion), calls=%async_computation.2 | async-start | bytes 3407872 | tf_op jit(solution)/shard_map/all_to_all | solution.py:304
  114.2 83.8 %reduce-scatter.2.cloned.1.call-start = ((), (), s32[]{:S(2)}) async-start(), calls=%async_computation.6 | async-start | bytes 3096576 | tf_op jit(solution)/shard_map/reduce_scatter | solution.py:307
  114.2 4.8 %collective-permute-start.7 = (bf16[32,128,128]{2,1,0:T(8,128)(2,1)S(1)}, bf16[32,128,128]{2,1,0:T(8,128)(2,1)}, u32[]{:S(2)}, u32[]{:S(2)}) collective-permute-start(bf16[32,128,128]{2,1,0:T(8,128)(2,1)S(1)} %all-to-all-done.1.own), channel_id=1, source_target_pairs={{0,1},{1,0},{2,3},{3,2},{4,5},{5,4},{6,7},{7,6},{8,9},{9,8},{10,11... | collective-permute-start | bytes 3145736 | tf_op jit(solution)/shard_map/ppermute | solution.py:273
  119.1 1.7 copy-start.3
  157.6 18.6 %all-to-all-start.3 = ((bf16[8,192,128]{2,1,0:T(8,128)(2,1)}), bf16[8,192,128]{2,1,0:T(8,128)(2,1)S(1)}, u32[]{:S(2)}, u32[]{:S(2)}) async-start(bf16[8,192,128]{2,1,0:T(8,128)(2,1)} %bitcast.9), calls=%async_computation.4 | async-start | bytes 786432 | tf_op jit(solution)/shard_map/all_to_all | solution.py:309
Sparse Core Ops, SparseCore 0:
  69.8 34.2 all-gather.3
  156.9 38.3 reduce-scatter.1

commit v4 on v3

--- a/solution.py
+++ b/solution.py
@@ -51,63 +51,71 @@
     )(weights, patterns, inverse)
 
 
-def join_kernel(*refs):
+def sort_kernel(where, *refs):
+    came, panels, slices = refs[:NY], refs[NY], refs[NY + 1 :]
     for s in range(NY):
-        refs[NY][s * 144 : (s + 1) * 144, :] = refs[s][...]
-
-
-def join(came):
-    return pl.pallas_call(
-        join_kernel,
-        out_shape=jax.ShapeDtypeStruct((NY * 144, 128), bf16),
-        in_specs=[VMEM] * NY,
-        out_specs=VMEM,
+        panels[s * 144 : (s + 1) * 144, :] = came[s][512:656, :]
+        for step in range(NX):
+            at = pl.multiple_of(lax.rem(where[0] + step, NX) * 128, 128)
+            slices[step][s] = came[s][pl.ds(at, 128), :]
+
+
+def sort(where, came):
+    return pl.pallas_call(
+        sort_kernel,
+        out_shape=(jax.ShapeDtypeStruct((NY * 144, 128), bf16),)
+        + (jax.ShapeDtypeStruct((NY, 128, 128), bf16),) * NX,
+        in_specs=[SMEM] + [VMEM] * NY,
+        out_specs=(VMEM,) * (1 + NX),
         compiler_params=pltpu.CompilerParams(vmem_limit_bytes=16 * 1024 * 1024),
-    )(*came)
-
-
-def prep_kernel(tokens, routes, blocks, panel):
+    )(where, *came)
+
+
+def prep_kernel(tokens, routes, blocks):
     squares = jnp.zeros((128, 128), f32)
     for s in range(32):
         part = tokens[:, s * 128 : (s + 1) * 128]
-        blocks[s] = part
+        blocks[s // NX, (s % NX) * 128 : (s % NX) * 128 + 128, :] = part
         wide = part.astype(f32)
         squares = squares + wide * wide
-    panel[0:128, :] = tokens[:, 0:128].astype(f32).T.astype(bf16)
+    turned = tokens[:, 0:128].astype(f32).T.astype(bf16)
     norms = jnp.sum(squares.T, axis=0, keepdims=True) * (1.0 / D)
     high = norms.astype(bf16).astype(f32)
     named = jnp.concatenate(
         [routes[...].astype(f32), jnp.zeros((128, 120), f32)], axis=1
     ).T
-    panel[128:144, :] = jnp.concatenate(
+    notes = jnp.concatenate(
         [named[0:8], high, norms - high, jnp.zeros((6, 128), f32)], axis=0
     ).astype(bf16)
+    for s in range(NY):
+        blocks[s, 512:640, :] = turned
+        blocks[s, 640:656, :] = notes
 
 
 def prepare(tokens, routes):
     return pl.pallas_call(
         prep_kernel,
-        out_shape=(
-            jax.ShapeDtypeStruct((32, 128, 128), bf16),
-            jax.ShapeDtypeStruct((144, 128), bf16),
-        ),
+        out_shape=jax.ShapeDtypeStruct((NY, 656, 128), bf16),
         in_specs=[VMEM] * 2,
-        out_specs=(VMEM,) * 2,
+        out_specs=VMEM,
         compiler_params=pltpu.CompilerParams(vmem_limit_bytes=16 * 1024 * 1024),
     )(tokens, routes)
 
 
-def gram_kernel(where, wanted, own, other, panels, out, left_all, right, squares, marks, left, total, norms):
-    x, c, y = where[0], where[1], where[2]
+def gram_kernel(where, wanted, *refs):
+    parts, panels, out = refs[: 2 * NX], refs[2 * NX], refs[2 * NX + 1]
+    left_all, right, squares, marks, left, total, norms = refs[2 * NX + 2 :]
+    x, c = where[0], where[1]
     ids = wanted[...]
     norms[...] = jnp.zeros_like(norms)
-    for half, source in ((0, own), (1, other)):
-        core = c if half == 0 else 1 - c
-
-        @pl.loop(0, HELD)
-        def _(b):
-            place = ((b % NX) * NC + core) * NY + lax.rem(y - b // NX + NY, NY)
-            at = pl.ds(pl.multiple_of((half * HELD + b) * 128, 128), 128)
+    for number, source in enumerate(parts):
+        core = c if number < NX else 1 - c
+        first = (lax.rem(x - number % NX + NX, NX) * NC + core) * NY
+
+        @pl.loop(0, NY)
+        def _(b, number=number, source=source, first=first):
+            place = first + b
+            at = pl.ds(pl.multiple_of((number * NY + b) * 128, 128), 128)
             turned = panels[place, 0:128, :]
             notes = panels[place, 128:144, :].astype(f32)
             left_all[:, at] = turned
@@ -163,11 +171,11 @@
         )
 
 
-def gram(where, wanted, own, other, panels):
+def gram(where, wanted, parts, panels):
     return pl.pallas_call(
         gram_kernel,
         out_shape=jax.ShapeDtypeStruct((HELD, ROWS, 128), f32),
-        in_specs=[SMEM] + [VMEM] * 4,
+        in_specs=[SMEM] + [VMEM] * (2 + 2 * NX),
         out_specs=VMEM,
         scratch_shapes=[
             pltpu.VMEM((128, 8192), bf16),
@@ -182,7 +190,7 @@
         cost_estimate=pl.CostEstimate(
             flops=2 * 4096 * 8192 * 256, bytes_accessed=8 << 20, transcendentals=0
         ),
-    )(where, wanted, own, other, panels)
+    )(where, wanted, *parts, panels)
 
 
 def parts_of(value, count):
@@ -294,16 +302,21 @@
         lax.dynamic_slice_in_dim(inverse[0], y * 16, 16, 0),
     )
     spread = lax.all_to_all(pieces, EXPERT, 0, 0, tiled=True)
-    blocks, panel = prepare(tokens, routes)
-    came = [panel] + [swap(panel, "y", NY, step) for step in range(1, NY)]
+    blocks = prepare(tokens, routes)
+
+    def block(step):
+        return lax.dynamic_index_in_dim(blocks, (y + step) % NY, 0, keepdims=False)
+
+    came = [block(0)] + [swap(block(step), "y", NY, step) for step in range(1, NY)]
     spread, *came = lax.optimization_barrier((spread, *came))
-    panels = lax.all_gather(join(came), ("x", "c"), axis=0, tiled=False).reshape(64, 144, 128)
-    own = lax.all_to_all(after(blocks, spread), ("y", "x"), 0, 0, tiled=True)
-    other = swap(own, "c", NC, 1)
+    panels, *parts = sort(where, came)
+    panels = lax.all_gather(panels, ("x", "c"), axis=0, tiled=False).reshape(64, 144, 128)
     spread = jnp.take(spread, source, axis=0, mode="clip")
-    held = lax.all_to_all(after(spread, own), EXPERT, 0, 0, tiled=True)
-
-    sums = gram(where, wanted, own, other, panels)
+    held = lax.all_to_all(spread, EXPERT, 0, 0, tiled=True)
+    parts = parts[:1] + [swap(parts[step], "x", NX, step) for step in range(1, NX)]
+    parts = parts + [swap(part, "c", NC, 1) for part in parts]
+
+    sums = gram(where, wanted, parts, panels)
     sums = lax.psum_scatter(after(sums, held), "z", scatter_dimension=0, tiled=True)
     moved = held[0:16, 0:96].reshape(NY, 192, 128)
     moved = lax.all_to_all(moved, "y", 0, 0, tiled=True)[0]

time: 226 us -> 243 us (1.075)
  starting transfers between devices: 66.4 us -> 80.5 us
  waiting for transfers between devices: 55.6 us -> 59.7 us
    ppermute x8 -> x14, waiting for transfers between devices: 3.97 us -> 44.5 us  [swap(): lax.ppermute(value, axis, [(i, (i + step) % size) for i in range(size)])]
    all_to_all x2 -> x1, waiting for transfers between devices: 26 us -> 0.01 us  [shards(): held = lax.all_to_all(spread, EXPERT, 0, 0, tiled=True)]
    ppermute x8 -> x14, starting transfers between devices: 30.9 us -> 49.4 us  [swap(): lax.ppermute(value, axis, [(i, (i + step) % size) for i in range(size)])]
    all_to_all x1, waiting for transfers between devices: 10.5 us -> 0.01 us  [shards(): spread = lax.all_to_all(pieces, EXPERT, 0, 0, tiled=True)]
    all_to_all x2 -> x1, starting transfers between devices: 17 us -> 11.2 us  [shards(): held = lax.all_to_all(spread, EXPERT, 0, 0, tiled=True)]
  transfers between devices with their start and end apart: 14 -> 19, of which waited for: 6 -> 8; matrix products, arithmetic and copies ran while one was open for 2% -> 2% of each run, Pallas kernels for 16% -> 14%
where the time goes in v4:
time: 243 us; the launch traced here: 238 us
  starting transfers between devices  80.5 us (33%)
  waiting for transfers between devices  59.7 us (25%)
  Pallas kernels  43.5 us (18%)
  blocking collectives  31 us (13%)
  between operations  13.8 us (6%)
  local copies, waits for them, and re-layouts  9.76 us (4%)
    ppermute x14, starting transfers between devices, swap(): lax.ppermute(value, axis, [(i, (i + step) % size) for i in range(size)])  49.4 us
    ppermute x14, waiting for transfers between devices, swap(): lax.ppermute(value, axis, [(i, (i + step) % size) for i in range(size)])  44.5 us
    pallas_call x1, Pallas kernels, gram(): pl.pallas_call(gram_kernel, out_shape=jax.ShapeDtypeStruct((HELD, ROWS, 1...  32.4 us
    all_gather x1, blocking collectives, shards(): shared = lax.all_gather(shared, 'y', axis=0, tiled=False)  21.6 us
    all_to_all x1, waiting for transfers between devices, shards(): moved = lax.all_to_all(moved, 'y', 0, 0, tiled=True)[0]  15.1 us
    all_to_all x1, starting transfers between devices, shards(): spread = lax.all_to_all(pieces, EXPERT, 0, 0, tiled=True)  15.1 us
    all_to_all x1, starting transfers between devices, shards(): held = lax.all_to_all(spread, EXPERT, 0, 0, tiled=True)  11.2 us
    all_to_all x1, blocking collectives, shards(): sums = lax.all_to_all(after(sums, shared), 'x', 0, 0, tiled=True)  9.39 us
  transfers between devices with their start and end apart: 19, of which 8 were waited for; matrix products, arithmetic and copies ran while one was open for 2% of the time, Pallas kernels for 14%

profile of v4, /device:TPU:1, one launch (start us, length us, event | category | flops | bytes accessed | tf_op | source)
XLA Modules:
  0.0 238.5 jit_solution(13438949828822014845)
XLA Ops:
  8.3 1.4 copy-done.1
  9.8 1.5 shard_map.73
  11.3 15.1 %all-to-all-start = ((bf16[64,104,128]{2,1,0:T(8,128)(2,1)}), bf16[64,104,128]{2,1,0:T(8,128)(2,1)}, u32[]{:S(2)}, u32[]{:S(2)}) async-start(bf16[64,104,128]{2,1,0:T(8,128)(2,1)} %shard_map.73), calls=%async_computation | async-start | bytes 3407872 | tf_op jit(solution)/shard_map/all_to_all | solution.py:304
  27.3 3.2 %collective-permute-start = (bf16[656,128]{1,0:T(8,128)(2,1)S(1)}, bf16[656,128]{1,0:T(8,128)(2,1)S(1)}, u32[]{:S(2)}, u32[]{:S(2)}) collective-permute-start(bf16[656,128]{1,0:T(8,128)(2,1)S(1)} %get-tuple-element.43), channel_id=1, source_target_pairs={{0,64},{64,128},{128,192},{192,256},{256,320},{320,384},{384,448},... | collective-permute-start | bytes 503816 | tf_op jit(solution)/shard_map/ppermute | solution.py:281
  30.5 4.2 %collective-permute-start.1 = (bf16[656,128]{1,0:T(8,128)(2,1)S(1)}, bf16[656,128]{1,0:T(8,128)(2,1)S(1)}, u32[]{:S(2)}, u32[]{:S(2)}) collective-permute-start(bf16[656,128]{1,0:T(8,128)(2,1)S(1)} %get-tuple-element.42), channel_id=1, source_target_pairs={{0,128},{64,192},{128,256},{192,320},{256,384},{320,448},{384,0},{... | collective-permute-start | bytes 503816 | tf_op jit(solution)/shard_map/ppermute | solution.py:281
  34.7 4.6 %collective-permute-start.2 = (bf16[656,128]{1,0:T(8,128)(2,1)S(1)}, bf16[656,128]{1,0:T(8,128)(2,1)S(1)}, u32[]{:S(2)}, u32[]{:S(2)}) collective-permute-start(bf16[656,128]{1,0:T(8,128)(2,1)S(1)} %get-tuple-element.41), channel_id=1, source_target_pairs={{0,192},{64,256},{128,320},{192,384},{256,448},{320,0},{384,64},{4... | collective-permute-start | bytes 503816 | tf_op jit(solution)/shard_map/ppermute | solution.py:281
  39.4 3.5 %collective-permute-start.3 = (bf16[656,128]{1,0:T(8,128)(2,1)S(1)}, bf16[656,128]{1,0:T(8,128)(2,1)S(1)}, u32[]{:S(2)}, u32[]{:S(2)}) collective-permute-start(bf16[656,128]{1,0:T(8,128)(2,1)S(1)} %get-tuple-element.40), channel_id=1, source_target_pairs={{0,256},{64,320},{128,384},{192,448},{256,0},{320,64},{384,128},{4... | collective-permute-start | bytes 503816 | tf_op jit(solution)/shard_map/ppermute | solution.py:281
  42.9 4.9 %collective-permute-start.4 = (bf16[656,128]{1,0:T(8,128)(2,1)S(1)}, bf16[656,128]{1,0:T(8,128)(2,1)S(1)}, u32[]{:S(2)}, u32[]{:S(2)}) collective-permute-start(bf16[656,128]{1,0:T(8,128)(2,1)S(1)} %get-tuple-element.39), channel_id=1, source_target_pairs={{0,320},{64,384},{128,448},{192,0},{256,64},{320,128},{384,192},{4... | collective-permute-start | bytes 503816 | tf_op jit(solution)/shard_map/ppermute | solution.py:281
  47.8 5.0 %collective-permute-start.5 = (bf16[656,128]{1,0:T(8,128)(2,1)S(1)}, bf16[656,128]{1,0:T(8,128)(2,1)S(1)}, u32[]{:S(2)}, u32[]{:S(2)}) collective-permute-start(bf16[656,128]{1,0:T(8,128)(2,1)S(1)} %get-tuple-element.38), channel_id=1, source_target_pairs={{0,384},{64,448},{128,0},{192,64},{256,128},{320,192},{384,256},{4... | collective-permute-start | bytes 503816 | tf_op jit(solution)/shard_map/ppermute | solution.py:281
  52.8 3.0 %collective-permute-start.6 = (bf16[656,128]{1,0:T(8,128)(2,1)S(1)}, bf16[656,128]{1,0:T(8,128)(2,1)S(1)}, u32[]{:S(2)}, u32[]{:S(2)}) collective-permute-start(bf16[656,128]{1,0:T(8,128)(2,1)S(1)} %get-tuple-element.37), channel_id=1, source_target_pairs={{0,448},{64,0},{128,64},{192,128},{256,192},{320,256},{384,320},{4... | collective-permute-start | bytes 503816 | tf_op jit(solution)/shard_map/ppermute | solution.py:281
  55.9 4.0 %collective-permute-done.3.refs_4_ = bf16[656,128]{1,0:T(8,128)(2,1)S(1)} collective-permute-done((bf16[656,128]{1,0:T(8,128)(2,1)S(1)}, bf16[656,128]{1,0:T(8,128)(2,1)S(1)}, u32[]{:S(2)}, u32[]{:S(2)}) %collective-permute-start.3) | collective-permute-done | bytes 167968 | tf_op jit(solution)/shard_map/ppermute | solution.py:281
  59.9 4.9 %collective-permute-done.4.refs_5_ = bf16[656,128]{1,0:T(8,128)(2,1)S(1)} collective-permute-done((bf16[656,128]{1,0:T(8,128)(2,1)S(1)}, bf16[656,128]{1,0:T(8,128)(2,1)S(1)}, u32[]{:S(2)}, u32[]{:S(2)}) %collective-permute-start.4) | collective-permute-done | bytes 167968 | tf_op jit(solution)/shard_map/ppermute | solution.py:281
  64.8 7.3 %collective-permute-done.5.refs_6_ = bf16[656,128]{1,0:T(8,128)(2,1)S(1)} collective-permute-done((bf16[656,128]{1,0:T(8,128)(2,1)S(1)}, bf16[656,128]{1,0:T(8,128)(2,1)S(1)}, u32[]{:S(2)}, u32[]{:S(2)}) %collective-permute-start.5) | collective-permute-done | bytes 167968 | tf_op jit(solution)/shard_map/ppermute | solution.py:281
  73.3 1.5 shard_map.75
  75.1 3.5 %gather_fusion = bf16[64,104,128]{2,1,0:T(8,128)(2,1)} fusion(bf16[64,104,128]{2,1,0:T(8,128)(2,1)} %all-to-all-done, s32[1024]{0:T(1024)S(1)} %pad_clamp_fusion), kind=kCustom, calls=%fused_computation | custom fusion | bytes 3408128 | tf_op jit(solution)/shard_map/jit(_take)/gather | solution.py:314
  78.5 11.2 %all-to-all-start.1 = ((bf16[64,104,128]{2,1,0:T(8,128)(2,1)}), bf16[64,104,128]{2,1,0:T(8,128)(2,1)S(1)}, u32[]{:S(2)}, u32[]{:S(2)}) async-start(bf16[64,104,128]{2,1,0:T(8,128)(2,1)} %gather_fusion), calls=%async_computation.1 | async-start | bytes 3407872 | tf_op jit(solution)/shard_map/all_to_all | solution.py:315
  89.8 3.3 %collective-permute-start.7 = (bf16[8,128,128]{2,1,0:T(8,128)(2,1)}, bf16[8,128,128]{2,1,0:T(8,128)(2,1)S(1)}, u32[]{:S(2)}, u32[]{:S(2)}) collective-permute-start(bf16[8,128,128]{2,1,0:T(8,128)(2,1)} %get-tuple-element.30), channel_id=1, source_target_pairs={{0,16},{16,32},{32,48},{48,0},{1,17},{17,33},{33,49},{49,1},{2,18}... | collective-permute-start | bytes 786440 | tf_op jit(solution)/shard_map/ppermute | solution.py:281
  93.1 4.5 %collective-permute-start.8 = (bf16[8,128,128]{2,1,0:T(8,128)(2,1)}, bf16[8,128,128]{2,1,0:T(8,128)(2,1)S(1)}, u32[]{:S(2)}, u32[]{:S(2)}) collective-permute-start(bf16[8,128,128]{2,1,0:T(8,128)(2,1)} %get-tuple-element.31), channel_id=1, source_target_pairs={{0,32},{16,48},{32,0},{48,16},{1,33},{17,49},{33,1},{49,17},{2,34}... | collective-permute-start | bytes 786440 | tf_op jit(solution)/shard_map/ppermute | solution.py:281
  97.6 3.0 %collective-permute-start.9 = (bf16[8,128,128]{2,1,0:T(8,128)(2,1)S(1)}, bf16[8,128,128]{2,1,0:T(8,128)(2,1)S(1)}, u32[]{:S(2)}, u32[]{:S(2)}) collective-permute-start(bf16[8,128,128]{2,1,0:T(8,128)(2,1)S(1)} %get-tuple-element.32), channel_id=1, source_target_pairs={{0,48},{16,0},{32,16},{48,32},{1,49},{17,1},{33,17},{49,33},{2,50}... | collective-permute-start | bytes 786440 | tf_op jit(solution)/shard_map/ppermute | solution.py:281
  100.6 3.1 %collective-permute-start.10 = (bf16[8,128,128]{2,1,0:T(8,128)(2,1)S(1)}, bf16[8,128,128]{2,1,0:T(8,128)(2,1)S(1)}, u32[]{:S(2)}, u32[]{:S(2)}) collective-permute-start(bf16[8,128,128]{2,1,0:T(8,128)(2,1)S(1)} %get-tuple-element.29.refs_0_), channel_id=1, source_target_pairs={{0,1},{1,0},{2,3},{3,2},{4,5},{5,4},{6,7},{7,6},{8,9},{9,8},{10,11... | collective-permute-start | bytes 786440 | tf_op jit(solution)/shard_map/ppermute | solution.py:281
  103.8 14.6 %collective-permute-done.7.refs_1_ = bf16[8,128,128]{2,1,0:T(8,128)(2,1)S(1)} collective-permute-done((bf16[8,128,128]{2,1,0:T(8,128)(2,1)}, bf16[8,128,128]{2,1,0:T(8,128)(2,1)S(1)}, u32[]{:S(2)}, u32[]{:S(2)}) %collective-permute-start.7) | collective-permute-done | bytes 262176 | tf_op jit(solution)/shard_map/ppermute | solution.py:281
  118.3 2.7 %collective-permute-start.11 = (bf16[8,128,128]{2,1,0:T(8,128)(2,1)S(1)}, bf16[8,128,128]{2,1,0:T(8,128)(2,1)}, u32[]{:S(2)}, u32[]{:S(2)}) collective-permute-start(bf16[8,128,128]{2,1,0:T(8,128)(2,1)S(1)} %collective-permute-done.7.refs_1_), channel_id=1, source_target_pairs={{0,1},{1,0},{2,3},{3,2},{4,5},{5,4},{6,7},{7,6},{8,9},{9,8},{10,11... | collective-permute-start | bytes 786440 | tf_op jit(solution)/shard_map/ppermute | solution.py:281
  121.1 11.3 %collective-permute-done.8.refs_2_ = bf16[8,128,128]{2,1,0:T(8,128)(2,1)S(1)} collective-permute-done((bf16[8,128,128]{2,1,0:T(8,128)(2,1)}, bf16[8,128,128]{2,1,0:T(8,128)(2,1)S(1)}, u32[]{:S(2)}, u32[]{:S(2)}) %collective-permute-start.8) | collective-permute-done | bytes 262176 | tf_op jit(solution)/shard_map/ppermute | solution.py:281
  132.4 2.3 collective-permute-start.12
  134.8 2.0 collective-permute-start.13
  138.3 1.7 copy-done.3
  140.0 32.4 %shard_map.76 = f32[32,168,128]{2,1,0:T(8,128)} custom-call(s32[3]{0:T(128)S(1)} %pad_add_fusion.where, f32[32,128]{1,0:T(8,128)S(1)} %broadcast_in_dim.28.wanted, bf16[8,128,128]{2,1,0:T(8,128)(2,1)S(1)} %get-tuple-element.29.refs_0_, bf16[8,128,128]{2,1,0:T(8,128)(2,1)S(1)} %collective-permute-done.7.refs_1_, ...), custom_call_target="tpu_custom_call" | custom-call | flops 17179869184 | bytes 8388608 | tf_op jit(solution)/shard_map/pallas_call | solution.py:175
  173.1 4.7 %all-to-all-start.2 = ((bf16[8,192,128]{2,1,0:T(8,128)(2,1)}), bf16[8,192,128]{2,1,0:T(8,128)(2,1)S(1)}, u32[]{:S(2)}, u32[]{:S(2)}) async-start(bf16[8,192,128]{2,1,0:T(8,128)(2,1)} %bitcast.17), calls=%async_computation.3 | async-start | bytes 786432 | tf_op jit(solution)/shard_map/all_to_all | solution.py:322
  177.8 15.1 %all-to-all-done.2 = bf16[8,192,128]{2,1,0:T(8,128)(2,1)S(1)} async-done(((bf16[8,192,128]{2,1,0:T(8,128)(2,1)}), bf16[8,192,128]{2,1,0:T(8,128)(2,1)S(1)}, u32[]{:S(2)}, u32[]{:S(2)}) %all-to-all-start.2) | async-done | bytes 393248 | tf_op jit(solution)/shard_map/all_to_all | solution.py:322
  192.9 21.6 %all-gather.1 = bf16[2304,128]{1,0:T(8,128)(2,1)S(1)} all-gather(bf16[288,128]{1,0:T(8,128)(2,1)S(1)} %pad_maximum_fusion), channel_id=3, replica_groups=mesh['y'=8,'x'=4,'z'=8,'c'=2] {'y'}, dimensions={0}, use_global_device_ids=true | all-gather | bytes 663552 | tf_op jit(solution)/shard_map/all_gather | solution.py:324
  214.6 9.4 %all_to_all.20.total = f32[4,168,128]{2,1,0:T(8,128)S(1)} all-to-all(f32[4,168,128]{2,1,0:T(8,128)} %reduce-scatter.2.cloned.1.call-done), channel_id=1, replica_groups=mesh['y'=8,'x'=4,'z'=8,'c'=2] {'x'}, dimensions={0} | all-to-all | bytes 688128 | tf_op jit(solution)/shard_map/all_to_all | solution.py:325
  224.0 7.7 %shard_map.77 = bf16[1536,512]{1,0:T(8,128)(2,1)} custom-call(s32[3]{0:T(128)S(1)} %pad_add_fusion.where, f32[4,168,128]{2,1,0:T(8,128)S(1)} %all_to_all.20.total, bf16[8,288,128]{2,1,0:T(8,128)(2,1)S(1)} %bitcast.33, bf16[64,104,128]{2,1,0:T(8,128)(2,1)S(1)} %all-to-all-done.1.held), custom_call_target="tpu_custom_call" | custom-call | tf_op jit(solution)/shard_map/pallas_call | solution.py:266
  (47 shorter events, 6.3 us)
Async XLA Ops:
  6.5 0.9 copy-start
  8.3 1.4 copy-start.1
  11.3 15.3 %copy-start.4 = (s32[128,8]{0,1:T(8,128)S(1)}, s32[128,8]{0,1:T(8,128)}, u32[]{:S(2)}) copy-start(s32[128,8]{0,1:T(8,128)} %param.8) | copy-start | bytes 12292
  11.3 15.4 %copy-start.2 = (bf16[128,4096]{1,0:T(8,128)(2,1)S(1)}, bf16[128,4096]{1,0:T(8,128)(2,1)}, u32[]{:S(2)}) copy-start(bf16[128,4096]{1,0:T(8,128)(2,1)} %tokens.1) | copy-start | bytes 3145732
  11.3 62.0 %all-to-all-start = ((bf16[64,104,128]{2,1,0:T(8,128)(2,1)}), bf16[64,104,128]{2,1,0:T(8,128)(2,1)}, u32[]{:S(2)}, u32[]{:S(2)}) async-start(bf16[64,104,128]{2,1,0:T(8,128)(2,1)} %shard_map.73), calls=%async_computation | async-start | bytes 3407872 | tf_op jit(solution)/shard_map/all_to_all | solution.py:304
  26.4 111.8 %all-gather.4.cloned.1.call-start = ((), (), s32[]{:S(2)}) async-start(), calls=%async_computation.6 | async-start | bytes 2654208 | tf_op jit(solution)/shard_map/all_gather | solution.py:313
  27.1 47.7 %copy-start.5 = (s32[64]{0:T(128)S(1)}, s32[64]{0:T(128)}, u32[]{:S(2)}) copy-start(s32[64]{0:T(128)} %param.10) | copy-start | bytes 772
  27.1 47.7 %copy-start.6 = (s32[64]{0:T(128)S(1)}, s32[64]{0:T(128)}, u32[]{:S(2)}) copy-start(s32[64]{0:T(128)} %param.9) | copy-start | bytes 772
  27.3 20.5 %collective-permute-start = (bf16[656,128]{1,0:T(8,128)(2,1)S(1)}, bf16[656,128]{1,0:T(8,128)(2,1)S(1)}, u32[]{:S(2)}, u32[]{:S(2)}) collective-permute-start(bf16[656,128]{1,0:T(8,128)(2,1)S(1)} %get-tuple-element.43), channel_id=1, source_target_pairs={{0,64},{64,128},{128,192},{192,256},{256,320},{320,384},{384,448},... | collective-permute-start | bytes 503816 | tf_op jit(solution)/shard_map/ppermute | solution.py:281
  30.5 22.3 %collective-permute-start.1 = (bf16[656,128]{1,0:T(8,128)(2,1)S(1)}, bf16[656,128]{1,0:T(8,128)(2,1)S(1)}, u32[]{:S(2)}, u32[]{:S(2)}) collective-permute-start(bf16[656,128]{1,0:T(8,128)(2,1)S(1)} %get-tuple-element.42), channel_id=1, source_target_pairs={{0,128},{64,192},{128,256},{192,320},{256,384},{320,448},{384,0},{... | collective-permute-start | bytes 503816 | tf_op jit(solution)/shard_map/ppermute | solution.py:281
  34.7 21.1 %collective-permute-start.2 = (bf16[656,128]{1,0:T(8,128)(2,1)S(1)}, bf16[656,128]{1,0:T(8,128)(2,1)S(1)}, u32[]{:S(2)}, u32[]{:S(2)}) collective-permute-start(bf16[656,128]{1,0:T(8,128)(2,1)S(1)} %get-tuple-element.41), channel_id=1, source_target_pairs={{0,192},{64,256},{128,320},{192,384},{256,448},{320,0},{384,64},{4... | collective-permute-start | bytes 503816 | tf_op jit(solution)/shard_map/ppermute | solution.py:281
  39.4 20.5 %collective-permute-start.3 = (bf16[656,128]{1,0:T(8,128)(2,1)S(1)}, bf16[656,128]{1,0:T(8,128)(2,1)S(1)}, u32[]{:S(2)}, u32[]{:S(2)}) collective-permute-start(bf16[656,128]{1,0:T(8,128)(2,1)S(1)} %get-tuple-element.40), channel_id=1, source_target_pairs={{0,256},{64,320},{128,384},{192,448},{256,0},{320,64},{384,128},{4... | collective-permute-start | bytes 503816 | tf_op jit(solution)/shard_map/ppermute | solution.py:281
  42.9 21.9 %collective-permute-start.4 = (bf16[656,128]{1,0:T(8,128)(2,1)S(1)}, bf16[656,128]{1,0:T(8,128)(2,1)S(1)}, u32[]{:S(2)}, u32[]{:S(2)}) collective-permute-start(bf16[656,128]{1,0:T(8,128)(2,1)S(1)} %get-tuple-element.39), channel_id=1, source_target_pairs={{0,320},{64,384},{128,448},{192,0},{256,64},{320,128},{384,192},{4... | collective-permute-start | bytes 503816 | tf_op jit(solution)/shard_map/ppermute | solution.py:281
  47.8 24.4 %collective-permute-start.5 = (bf16[656,128]{1,0:T(8,128)(2,1)S(1)}, bf16[656,128]{1,0:T(8,128)(2,1)S(1)}, u32[]{:S(2)}, u32[]{:S(2)}) collective-permute-start(bf16[656,128]{1,0:T(8,128)(2,1)S(1)} %get-tuple-element.38), channel_id=1, source_target_pairs={{0,384},{64,448},{128,0},{192,64},{256,128},{320,192},{384,256},{4... | collective-permute-start | bytes 503816 | tf_op jit(solution)/shard_map/ppermute | solution.py:281
  52.8 20.5 %collective-permute-start.6 = (bf16[656,128]{1,0:T(8,128)(2,1)S(1)}, bf16[656,128]{1,0:T(8,128)(2,1)S(1)}, u32[]{:S(2)}, u32[]{:S(2)}) collective-permute-start(bf16[656,128]{1,0:T(8,128)(2,1)S(1)} %get-tuple-element.37), channel_id=1, source_target_pairs={{0,448},{64,0},{128,64},{192,128},{256,192},{320,256},{384,320},{4... | collective-permute-start | bytes 503816 | tf_op jit(solution)/shard_map/ppermute | solution.py:281
  78.5 93.8 %all-to-all-start.1 = ((bf16[64,104,128]{2,1,0:T(8,128)(2,1)}), bf16[64,104,128]{2,1,0:T(8,128)(2,1)S(1)}, u32[]{:S(2)}, u32[]{:S(2)}) async-start(bf16[64,104,128]{2,1,0:T(8,128)(2,1)} %gather_fusion), calls=%async_computation.1 | async-start | bytes 3407872 | tf_op jit(solution)/shard_map/all_to_all | solution.py:315
  89.8 124.8 %reduce-scatter.2.cloned.1.call-start = ((), (), s32[]{:S(2)}) async-start(), calls=%async_computation.5 | async-start | bytes 3096576 | tf_op jit(solution)/shard_map/reduce_scatter | solution.py:320
  89.8 28.5 %collective-permute-start.7 = (bf16[8,128,128]{2,1,0:T(8,128)(2,1)}, bf16[8,128,128]{2,1,0:T(8,128)(2,1)S(1)}, u32[]{:S(2)}, u32[]{:S(2)}) collective-permute-start(bf16[8,128,128]{2,1,0:T(8,128)(2,1)} %get-tuple-element.30), channel_id=1, source_target_pairs={{0,16},{16,32},{32,48},{48,0},{1,17},{17,33},{33,49},{49,1},{2,18}... | collective-permute-start | bytes 786440 | tf_op jit(solution)/shard_map/ppermute | solution.py:281
  93.1 39.3 %collective-permute-start.8 = (bf16[8,128,128]{2,1,0:T(8,128)(2,1)}, bf16[8,128,128]{2,1,0:T(8,128)(2,1)S(1)}, u32[]{:S(2)}, u32[]{:S(2)}) collective-permute-start(bf16[8,128,128]{2,1,0:T(8,128)(2,1)} %get-tuple-element.31), channel_id=1, source_target_pairs={{0,32},{16,48},{32,0},{48,16},{1,33},{17,49},{33,1},{49,17},{2,34}... | collective-permute-start | bytes 786440 | tf_op jit(solution)/shard_map/ppermute | solution.py:281
  97.6 37.1 %collective-permute-start.9 = (bf16[8,128,128]{2,1,0:T(8,128)(2,1)S(1)}, bf16[8,128,128]{2,1,0:T(8,128)(2,1)S(1)}, u32[]{:S(2)}, u32[]{:S(2)}) collective-permute-start(bf16[8,128,128]{2,1,0:T(8,128)(2,1)S(1)} %get-tuple-element.32), channel_id=1, source_target_pairs={{0,48},{16,0},{32,16},{48,32},{1,49},{17,1},{33,17},{49,33},{2,50}... | collective-permute-start | bytes 786440 | tf_op jit(solution)/shard_map/ppermute | solution.py:281
  100.6 36.5 %collective-permute-start.10 = (bf16[8,128,128]{2,1,0:T(8,128)(2,1)S(1)}, bf16[8,128,128]{2,1,0:T(8,128)(2,1)S(1)}, u32[]{:S(2)}, u32[]{:S(2)}) collective-permute-start(bf16[8,128,128]{2,1,0:T(8,128)(2,1)S(1)} %get-tuple-element.29.refs_0_), channel_id=1, source_target_pairs={{0,1},{1,0},{2,3},{3,2},{4,5},{5,4},{6,7},{7,6},{8,9},{9,8},{10,11... | collective-permute-start | bytes 786440 | tf_op jit(solution)/shard_map/ppermute | solution.py:281
  118.3 18.8 %collective-permute-start.11 = (bf16[8,128,128]{2,1,0:T(8,128)(2,1)S(1)}, bf16[8,128,128]{2,1,0:T(8,128)(2,1)}, u32[]{:S(2)}, u32[]{:S(2)}) collective-permute-start(bf16[8,128,128]{2,1,0:T(8,128)(2,1)S(1)} %collective-permute-done.7.refs_1_), channel_id=1, source_target_pairs={{0,1},{1,0},{2,3},{3,2},{4,5},{5,4},{6,7},{7,6},{8,9},{9,8},{10,11... | collective-permute-start | bytes 786440 | tf_op jit(solution)/shard_map/ppermute | solution.py:281
  132.4 4.7 %collective-permute-start.12 = (bf16[8,128,128]{2,1,0:T(8,128)(2,1)S(1)}, bf16[8,128,128]{2,1,0:T(8,128)(2,1)}, u32[]{:S(2)}, u32[]{:S(2)}) collective-permute-start(bf16[8,128,128]{2,1,0:T(8,128)(2,1)S(1)} %collective-permute-done.8.refs_2_), channel_id=1, source_target_pairs={{0,1},{1,0},{2,3},{3,2},{4,5},{5,4},{6,7},{7,6},{8,9},{9,8},{10,11... | collective-permute-start | bytes 786440 | tf_op jit(solution)/shard_map/ppermute | solution.py:281
  134.8 3.4 %collective-permute-start.13 = (bf16[8,128,128]{2,1,0:T(8,128)(2,1)S(1)}, bf16[8,128,128]{2,1,0:T(8,128)(2,1)S(1)}, u32[]{:S(2)}, u32[]{:S(2)}) collective-permute-start(bf16[8,128,128]{2,1,0:T(8,128)(2,1)S(1)} %collective-permute-done.9.refs_3_), channel_id=1, source_target_pairs={{0,1},{1,0},{2,3},{3,2},{4,5},{5,4},{6,7},{7,6},{8,9},{9,8},{10,11... | collective-permute-start | bytes 786440 | tf_op jit(solution)/shard_map/ppermute | solution.py:281
  138.3 1.7 copy-start.3
  173.1 19.8 %all-to-all-start.2 = ((bf16[8,192,128]{2,1,0:T(8,128)(2,1)}), bf16[8,192,128]{2,1,0:T(8,128)(2,1)S(1)}, u32[]{:S(2)}, u32[]{:S(2)}) async-start(bf16[8,192,128]{2,1,0:T(8,128)(2,1)} %bitcast.17), calls=%async_computation.3 | async-start | bytes 786432 | tf_op jit(solution)/shard_map/all_to_all | solution.py:322
Sparse Core Ops, SparseCore 0:
  75.0 53.4 all-gather.3
  172.5 40.0 reduce-scatter.1

commit v5 on v3

--- a/solution.py
+++ b/solution.py
@@ -127,26 +127,28 @@
 
     chunk = 2048
 
+    def build(g, k):
+        at = slice(k * chunk, (k + 1) * chunk)
+        hits = marks[pl.ds(pl.multiple_of(g * 8, 8), 8), at]
+        for j in range(8):
+            row = jnp.broadcast_to(hits[j : j + 1, :], (16, chunk)).astype(bf16)
+            for r in range(8):
+                left[k % 2, j * 128 + r * 16 : j * 128 + r * 16 + 16, :] = (
+                    left_all[r * 16 : r * 16 + 16, at] * row
+                )
+
+    build(0, 0)
+
     @pl.loop(0, 4)
     def _(g):
-        @pl.loop(0, 4)
-        def _(k):
-            at = pl.ds(pl.multiple_of(k * chunk, chunk), chunk)
-            hits = marks[pl.ds(pl.multiple_of(g * 8, 8), 8), at]
-            for j in range(8):
-                row = jnp.broadcast_to(hits[j : j + 1, :], (16, chunk)).astype(bf16)
-                for r in range(8):
-                    left[j * 128 + r * 16 : j * 128 + r * 16 + 16, :] = (
-                        left_all[r * 16 : r * 16 + 16, at] * row
-                    )
-            product = jnp.dot(left[...], right[at, :], preferred_element_type=f32)
-
-            @pl.when(k == 0)
-            def _():
+        for k in range(4):
+            product = jnp.dot(
+                left[k % 2], right[k * chunk : (k + 1) * chunk, :], preferred_element_type=f32
+            )
+            build(g if k < 3 else lax.rem(g + 1, 4), (k + 1) % 4)
+            if k == 0:
                 total[...] = product
-
-            @pl.when(k > 0)
-            def _():
+            else:
                 total[...] += product
 
         for j in range(8):
@@ -174,7 +176,7 @@
             pltpu.VMEM((8192, 256), bf16),
             pltpu.VMEM((8192, 256), bf16),
             pltpu.VMEM((HELD, 8192), f32),
-            pltpu.VMEM((1024, 2048), bf16),
+            pltpu.VMEM((2, 1024, 2048), bf16),
             pltpu.VMEM((1024, 256), f32),
             pltpu.VMEM((HELD, 128), f32),
         ],

time: 226 us -> 226 us (level)
  the two profiles are of different devices: /device:TPU:1 before, /device:TPU:64 now
where the time goes in v5:
time: 226 us; the launch traced here: 225 us
  starting transfers between devices  65.4 us (29%)
  waiting for transfers between devices  57.3 us (25%)
  Pallas kernels  41.3 us (18%)
  blocking collectives  36.9 us (16%)
  between operations  13.6 us (6%)
  local copies, waits for them, and re-layouts  10.2 us (5%)
    ppermute x8, starting transfers between devices, swap(): lax.ppermute(value, axis, [(i, (i + step) % size) for i in range(size)])  32.6 us
    pallas_call x1, Pallas kernels, gram(): pl.pallas_call(gram_kernel, out_shape=jax.ShapeDtypeStruct((HELD, ROWS, 1...  30 us
    all_gather x1, blocking collectives, shards(): shared = lax.all_gather(shared, 'y', axis=0, tiled=False)  25.6 us
    all_to_all x1, waiting for transfers between devices, shards(): own = lax.all_to_all(after(blocks, spread), ('y', 'x'), 0, 0, tiled=True)  24.9 us
    all_to_all x1, waiting for transfers between devices, shards(): moved = lax.all_to_all(moved, 'y', 0, 0, tiled=True)[0]  15.1 us
    all_to_all x1, starting transfers between devices, shards(): spread = lax.all_to_all(pieces, EXPERT, 0, 0, tiled=True)  13.1 us
    all_to_all x1, blocking collectives, shards(): sums = lax.all_to_all(after(sums, shared), 'x', 0, 0, tiled=True)  11.3 us
    all_to_all x1, starting transfers between devices, shards(): own = lax.all_to_all(after(blocks, spread), ('y', 'x'), 0, 0, tiled=True)  9.6 us
  transfers between devices with their start and end apart: 14, of which 6 were waited for; matrix products, arithmetic and copies ran while one was open for 2% of the time, Pallas kernels for 14%

profile of v5, /device:TPU:64, one launch (start us, length us, event | category | flops | bytes accessed | tf_op | source)
XLA Modules:
  0.0 224.9 jit_solution(14293706538298600686)
XLA Ops:
  6.5 0.9 copy-done
  7.6 0.7 dynamic-slice_bitcast_fusion.inverse
  8.3 1.4 copy-done.1
  9.8 1.5 shard_map.74
  11.3 13.1 %all-to-all-start = ((bf16[64,104,128]{2,1,0:T(8,128)(2,1)}), bf16[64,104,128]{2,1,0:T(8,128)(2,1)S(1)}, u32[]{:S(2)}, u32[]{:S(2)}) async-start(bf16[64,104,128]{2,1,0:T(8,128)(2,1)} %shard_map.74), calls=%async_computation | async-start | bytes 3407872 | tf_op jit(solution)/shard_map/all_to_all | solution.py:298
  24.6 1.3 shard_map.73
  25.9 3.6 %collective-permute-start = (bf16[144,128]{1,0:T(8,128)(2,1)S(1)}, bf16[144,128]{1,0:T(8,128)(2,1)S(1)}, u32[]{:S(2)}, u32[]{:S(2)}) collective-permute-start(bf16[144,128]{1,0:T(8,128)(2,1)S(1)} %get-tuple-element.24.refs_0_), channel_id=1, source_target_pairs={{0,64},{64,128},{128,192},{192,256},{256,320},{320,384},{384,448},... | collective-permute-start | bytes 110600 | tf_op jit(solution)/shard_map/ppermute | solution.py:275
  29.5 4.5 %collective-permute-start.1 = (bf16[144,128]{1,0:T(8,128)(2,1)S(1)}, bf16[144,128]{1,0:T(8,128)(2,1)S(1)}, u32[]{:S(2)}, u32[]{:S(2)}) collective-permute-start(bf16[144,128]{1,0:T(8,128)(2,1)S(1)} %get-tuple-element.24.refs_0_), channel_id=1, source_target_pairs={{0,128},{64,192},{128,256},{192,320},{256,384},{320,448},{384,0},{... | collective-permute-start | bytes 110600 | tf_op jit(solution)/shard_map/ppermute | solution.py:275
  34.0 4.9 %collective-permute-start.2 = (bf16[144,128]{1,0:T(8,128)(2,1)S(1)}, bf16[144,128]{1,0:T(8,128)(2,1)S(1)}, u32[]{:S(2)}, u32[]{:S(2)}) collective-permute-start(bf16[144,128]{1,0:T(8,128)(2,1)S(1)} %get-tuple-element.24.refs_0_), channel_id=1, source_target_pairs={{0,192},{64,256},{128,320},{192,384},{256,448},{320,0},{384,64},{4... | collective-permute-start | bytes 110600 | tf_op jit(solution)/shard_map/ppermute | solution.py:275
  38.9 3.8 %collective-permute-start.3 = (bf16[144,128]{1,0:T(8,128)(2,1)S(1)}, bf16[144,128]{1,0:T(8,128)(2,1)S(1)}, u32[]{:S(2)}, u32[]{:S(2)}) collective-permute-start(bf16[144,128]{1,0:T(8,128)(2,1)S(1)} %get-tuple-element.24.refs_0_), channel_id=1, source_target_pairs={{0,256},{64,320},{128,384},{192,448},{256,0},{320,64},{384,128},{4... | collective-permute-start | bytes 110600 | tf_op jit(solution)/shard_map/ppermute | solution.py:275
  42.7 5.2 %collective-permute-start.4 = (bf16[144,128]{1,0:T(8,128)(2,1)S(1)}, bf16[144,128]{1,0:T(8,128)(2,1)S(1)}, u32[]{:S(2)}, u32[]{:S(2)}) collective-permute-start(bf16[144,128]{1,0:T(8,128)(2,1)S(1)} %get-tuple-element.24.refs_0_), channel_id=1, source_target_pairs={{0,320},{64,384},{128,448},{192,0},{256,64},{320,128},{384,192},{4... | collective-permute-start | bytes 110600 | tf_op jit(solution)/shard_map/ppermute | solution.py:275
  47.9 5.3 %collective-permute-start.5 = (bf16[144,128]{1,0:T(8,128)(2,1)S(1)}, bf16[144,128]{1,0:T(8,128)(2,1)S(1)}, u32[]{:S(2)}, u32[]{:S(2)}) collective-permute-start(bf16[144,128]{1,0:T(8,128)(2,1)S(1)} %get-tuple-element.24.refs_0_), channel_id=1, source_target_pairs={{0,384},{64,448},{128,0},{192,64},{256,128},{320,192},{384,256},{4... | collective-permute-start | bytes 110600 | tf_op jit(solution)/shard_map/ppermute | solution.py:275
  53.2 3.3 %collective-permute-start.6 = (bf16[144,128]{1,0:T(8,128)(2,1)S(1)}, bf16[144,128]{1,0:T(8,128)(2,1)S(1)}, u32[]{:S(2)}, u32[]{:S(2)}) collective-permute-start(bf16[144,128]{1,0:T(8,128)(2,1)S(1)} %get-tuple-element.24.refs_0_), channel_id=1, source_target_pairs={{0,448},{64,0},{128,64},{192,128},{256,192},{320,256},{384,320},{4... | collective-permute-start | bytes 110600 | tf_op jit(solution)/shard_map/ppermute | solution.py:275
  56.5 2.5 %collective-permute-done.6.refs_7_ = bf16[144,128]{1,0:T(8,128)(2,1)S(1)} collective-permute-done((bf16[144,128]{1,0:T(8,128)(2,1)S(1)}, bf16[144,128]{1,0:T(8,128)(2,1)S(1)}, u32[]{:S(2)}, u32[]{:S(2)}) %collective-permute-start.6) | collective-permute-done | bytes 36896 | tf_op jit(solution)/shard_map/ppermute | solution.py:275
  59.0 7.1 %all-to-all-done = bf16[64,104,128]{2,1,0:T(8,128)(2,1)S(1)} async-done(((bf16[64,104,128]{2,1,0:T(8,128)(2,1)}), bf16[64,104,128]{2,1,0:T(8,128)(2,1)S(1)}, u32[]{:S(2)}, u32[]{:S(2)}) %all-to-all-start) | async-done | bytes 1703968 | tf_op jit(solution)/shard_map/all_to_all | solution.py:298
  66.2 0.8 shard_map.75
  67.0 0.6 copy-done.4
  67.5 9.6 %all-to-all-start.1 = ((bf16[32,128,128]{2,1,0:T(8,128)(2,1)}), bf16[32,128,128]{2,1,0:T(8,128)(2,1)S(1)}, u32[]{:S(2)}, u32[]{:S(2)}) async-start(bf16[32,128,128]{2,1,0:T(8,128)(2,1)} %get-tuple-element.23), calls=%async_computation.1 | async-start | bytes 2097152 | tf_op jit(solution)/shard_map/all_to_all | solution.py:303
  77.4 3.4 %gather_fusion = bf16[64,104,128]{2,1,0:T(8,128)(2,1)} fusion(bf16[64,104,128]{2,1,0:T(8,128)(2,1)} %copy-done.4, s32[1024]{0:T(1024)S(1)} %pad_clamp_fusion), kind=kCustom, calls=%fused_computation | custom fusion | bytes 3408128 | tf_op jit(solution)/shard_map/jit(_take)/gather | solution.py:305
  80.8 24.9 %all-to-all-done.1.own = bf16[32,128,128]{2,1,0:T(8,128)(2,1)S(1)} async-done(((bf16[32,128,128]{2,1,0:T(8,128)(2,1)}), bf16[32,128,128]{2,1,0:T(8,128)(2,1)S(1)}, u32[]{:S(2)}, u32[]{:S(2)}) %all-to-all-start.1) | async-done | bytes 1048608 | tf_op jit(solution)/shard_map/all_to_all | solution.py:303
  105.7 6.6 %all-to-all-start.2 = ((bf16[64,104,128]{2,1,0:T(8,128)(2,1)}), bf16[64,104,128]{2,1,0:T(8,128)(2,1)S(1)}, u32[]{:S(2)}, u32[]{:S(2)}) async-start(bf16[64,104,128]{2,1,0:T(8,128)(2,1)} %gather_fusion), calls=%async_computation.2 | async-start | bytes 3407872 | tf_op jit(solution)/shard_map/all_to_all | solution.py:306
  112.4 2.1 collective-permute-start.7
  114.9 2.2 collective-permute-done.7.other
  117.1 1.7 copy-done.3
  118.8 30.0 %shard_map.76 = f32[32,168,128]{2,1,0:T(8,128)} custom-call(s32[3]{0:T(128)S(1)} %pad_add_fusion.where, f32[32,128]{1,0:T(8,128)S(1)} %broadcast_in_dim.28.wanted, bf16[32,128,128]{2,1,0:T(8,128)(2,1)S(1)} %all-to-all-done.1.own, bf16[32,128,128]{2,1,0:T(8,128)(2,1)} %collective-permute-done.7.other, bf16[64,144,128]{2,1,0:T(8,128)(2,1)S(1)} %bitcast.20), custom_call_target="tpu_custom_call" | custom-call | flops 17179869184 | bytes 8388608 | tf_op jit(solution)/shard_map/pallas_call | solution.py:169
  148.8 5.3 %all-to-all-done.2.held = bf16[64,104,128]{2,1,0:T(8,128)(2,1)S(1)} async-done(((bf16[64,104,128]{2,1,0:T(8,128)(2,1)}), bf16[64,104,128]{2,1,0:T(8,128)(2,1)S(1)}, u32[]{:S(2)}, u32[]{:S(2)}) %all-to-all-start.2) | async-done | bytes 1703968 | tf_op jit(solution)/shard_map/all_to_all | solution.py:306
  154.1 0.8 slice.20
  154.9 3.5 %all-to-all-start.3 = ((bf16[8,192,128]{2,1,0:T(8,128)(2,1)}), bf16[8,192,128]{2,1,0:T(8,128)(2,1)S(1)}, u32[]{:S(2)}, u32[]{:S(2)}) async-start(bf16[8,192,128]{2,1,0:T(8,128)(2,1)} %bitcast.9), calls=%async_computation.4 | async-start | bytes 786432 | tf_op jit(solution)/shard_map/all_to_all | solution.py:311
  158.4 15.1 %all-to-all-done.3 = bf16[8,192,128]{2,1,0:T(8,128)(2,1)S(1)} async-done(((bf16[8,192,128]{2,1,0:T(8,128)(2,1)}), bf16[8,192,128]{2,1,0:T(8,128)(2,1)S(1)}, u32[]{:S(2)}, u32[]{:S(2)}) %all-to-all-start.3) | async-done | bytes 393248 | tf_op jit(solution)/shard_map/all_to_all | solution.py:311
  173.5 25.6 %all-gather.1 = bf16[2304,128]{1,0:T(8,128)(2,1)S(1)} all-gather(bf16[288,128]{1,0:T(8,128)(2,1)S(1)} %pad_maximum_fusion), channel_id=3, replica_groups=mesh['y'=8,'x'=4,'z'=8,'c'=2] {'y'}, dimensions={0}, use_global_device_ids=true | all-gather | bytes 663552 | tf_op jit(solution)/shard_map/all_gather | solution.py:313
  199.1 11.3 %all_to_all.25.total = f32[4,168,128]{2,1,0:T(8,128)S(1)} all-to-all(f32[4,168,128]{2,1,0:T(8,128)} %reduce-scatter.2.cloned.1.call-done), channel_id=1, replica_groups=mesh['y'=8,'x'=4,'z'=8,'c'=2] {'x'}, dimensions={0} | all-to-all | bytes 688128 | tf_op jit(solution)/shard_map/all_to_all | solution.py:314
  210.4 7.7 %shard_map.77 = bf16[1536,512]{1,0:T(8,128)(2,1)} custom-call(s32[3]{0:T(128)S(1)} %pad_add_fusion.where, f32[4,168,128]{2,1,0:T(8,128)S(1)} %all_to_all.25.total, bf16[8,288,128]{2,1,0:T(8,128)(2,1)S(1)} %bitcast.17, bf16[64,104,128]{2,1,0:T(8,128)(2,1)S(1)} %all-to-all-done.2.held), custom_call_target="tpu_custom_call" | custom-call | tf_op jit(solution)/shard_map/pallas_call | solution.py:260
  (38 shorter events, 1.1 us)
Async XLA Ops:
  6.5 0.9 copy-start
  8.3 1.4 copy-start.1
  11.3 13.2 %copy-start.5 = (s32[128,8]{0,1:T(8,128)S(1)}, s32[128,8]{0,1:T(8,128)}, u32[]{:S(2)}) copy-start(s32[128,8]{0,1:T(8,128)} %param.8) | copy-start | bytes 12292
  11.3 13.3 %copy-start.2 = (bf16[128,4096]{1,0:T(8,128)(2,1)S(1)}, bf16[128,4096]{1,0:T(8,128)(2,1)}, u32[]{:S(2)}) copy-start(bf16[128,4096]{1,0:T(8,128)(2,1)} %tokens.1) | copy-start | bytes 3145732
  11.3 54.9 %all-to-all-start = ((bf16[64,104,128]{2,1,0:T(8,128)(2,1)}), bf16[64,104,128]{2,1,0:T(8,128)(2,1)S(1)}, u32[]{:S(2)}, u32[]{:S(2)}) async-start(bf16[64,104,128]{2,1,0:T(8,128)(2,1)} %shard_map.74), calls=%async_computation | async-start | bytes 3407872 | tf_op jit(solution)/shard_map/all_to_all | solution.py:298
  24.4 92.7 %all-gather.4.cloned.1.call-start = ((), (), s32[]{:S(2)}) async-start(), calls=%async_computation.7 | async-start | bytes 2654208 | tf_op jit(solution)/shard_map/all_gather | solution.py:302
  25.9 51.3 %copy-start.6 = (s32[64]{0:T(128)S(1)}, s32[64]{0:T(128)}, u32[]{:S(2)}) copy-start(s32[64]{0:T(128)} %param.10) | copy-start | bytes 772
  25.9 51.3 %copy-start.7 = (s32[64]{0:T(128)S(1)}, s32[64]{0:T(128)}, u32[]{:S(2)}) copy-start(s32[64]{0:T(128)} %param.9) | copy-start | bytes 772
  25.9 22.0 %collective-permute-start = (bf16[144,128]{1,0:T(8,128)(2,1)S(1)}, bf16[144,128]{1,0:T(8,128)(2,1)S(1)}, u32[]{:S(2)}, u32[]{:S(2)}) collective-permute-start(bf16[144,128]{1,0:T(8,128)(2,1)S(1)} %get-tuple-element.24.refs_0_), channel_id=1, source_target_pairs={{0,64},{64,128},{128,192},{192,256},{256,320},{320,384},{384,448},... | collective-permute-start | bytes 110600 | tf_op jit(solution)/shard_map/ppermute | solution.py:275
  29.5 23.7 %collective-permute-start.1 = (bf16[144,128]{1,0:T(8,128)(2,1)S(1)}, bf16[144,128]{1,0:T(8,128)(2,1)S(1)}, u32[]{:S(2)}, u32[]{:S(2)}) collective-permute-start(bf16[144,128]{1,0:T(8,128)(2,1)S(1)} %get-tuple-element.24.refs_0_), channel_id=1, source_target_pairs={{0,128},{64,192},{128,256},{192,320},{256,384},{320,448},{384,0},{... | collective-permute-start | bytes 110600 | tf_op jit(solution)/shard_map/ppermute | solution.py:275
  34.0 22.5 %collective-permute-start.2 = (bf16[144,128]{1,0:T(8,128)(2,1)S(1)}, bf16[144,128]{1,0:T(8,128)(2,1)S(1)}, u32[]{:S(2)}, u32[]{:S(2)}) collective-permute-start(bf16[144,128]{1,0:T(8,128)(2,1)S(1)} %get-tuple-element.24.refs_0_), channel_id=1, source_target_pairs={{0,192},{64,256},{128,320},{192,384},{256,448},{320,0},{384,64},{4... | collective-permute-start | bytes 110600 | tf_op jit(solution)/shard_map/ppermute | solution.py:275
  38.9 17.5 %collective-permute-start.3 = (bf16[144,128]{1,0:T(8,128)(2,1)S(1)}, bf16[144,128]{1,0:T(8,128)(2,1)S(1)}, u32[]{:S(2)}, u32[]{:S(2)}) collective-permute-start(bf16[144,128]{1,0:T(8,128)(2,1)S(1)} %get-tuple-element.24.refs_0_), channel_id=1, source_target_pairs={{0,256},{64,320},{128,384},{192,448},{256,0},{320,64},{384,128},{4... | collective-permute-start | bytes 110600 | tf_op jit(solution)/shard_map/ppermute | solution.py:275
  42.7 13.7 %collective-permute-start.4 = (bf16[144,128]{1,0:T(8,128)(2,1)S(1)}, bf16[144,128]{1,0:T(8,128)(2,1)S(1)}, u32[]{:S(2)}, u32[]{:S(2)}) collective-permute-start(bf16[144,128]{1,0:T(8,128)(2,1)S(1)} %get-tuple-element.24.refs_0_), channel_id=1, source_target_pairs={{0,320},{64,384},{128,448},{192,0},{256,64},{320,128},{384,192},{4... | collective-permute-start | bytes 110600 | tf_op jit(solution)/shard_map/ppermute | solution.py:275
  47.9 8.6 %collective-permute-start.5 = (bf16[144,128]{1,0:T(8,128)(2,1)S(1)}, bf16[144,128]{1,0:T(8,128)(2,1)S(1)}, u32[]{:S(2)}, u32[]{:S(2)}) collective-permute-start(bf16[144,128]{1,0:T(8,128)(2,1)S(1)} %get-tuple-element.24.refs_0_), channel_id=1, source_target_pairs={{0,384},{64,448},{128,0},{192,64},{256,128},{320,192},{384,256},{4... | collective-permute-start | bytes 110600 | tf_op jit(solution)/shard_map/ppermute | solution.py:275
  53.2 5.9 %collective-permute-start.6 = (bf16[144,128]{1,0:T(8,128)(2,1)S(1)}, bf16[144,128]{1,0:T(8,128)(2,1)S(1)}, u32[]{:S(2)}, u32[]{:S(2)}) collective-permute-start(bf16[144,128]{1,0:T(8,128)(2,1)S(1)} %get-tuple-element.24.refs_0_), channel_id=1, source_target_pairs={{0,448},{64,0},{128,64},{192,128},{256,192},{320,256},{384,320},{4... | collective-permute-start | bytes 110600 | tf_op jit(solution)/shard_map/ppermute | solution.py:275
  66.2 1.4 copy-start.4
  67.5 38.2 %all-to-all-start.1 = ((bf16[32,128,128]{2,1,0:T(8,128)(2,1)}), bf16[32,128,128]{2,1,0:T(8,128)(2,1)S(1)}, u32[]{:S(2)}, u32[]{:S(2)}) async-start(bf16[32,128,128]{2,1,0:T(8,128)(2,1)} %get-tuple-element.23), calls=%async_computation.1 | async-start | bytes 2097152 | tf_op jit(solution)/shard_map/all_to_all | solution.py:303
  105.7 48.4 %all-to-all-start.2 = ((bf16[64,104,128]{2,1,0:T(8,128)(2,1)}), bf16[64,104,128]{2,1,0:T(8,128)(2,1)S(1)}, u32[]{:S(2)}, u32[]{:S(2)}) async-start(bf16[64,104,128]{2,1,0:T(8,128)(2,1)} %gather_fusion), calls=%async_computation.2 | async-start | bytes 3407872 | tf_op jit(solution)/shard_map/all_to_all | solution.py:306
  112.3 86.8 %reduce-scatter.2.cloned.1.call-start = ((), (), s32[]{:S(2)}) async-start(), calls=%async_computation.6 | async-start | bytes 3096576 | tf_op jit(solution)/shard_map/reduce_scatter | solution.py:309
  112.4 4.7 %collective-permute-start.7 = (bf16[32,128,128]{2,1,0:T(8,128)(2,1)S(1)}, bf16[32,128,128]{2,1,0:T(8,128)(2,1)}, u32[]{:S(2)}, u32[]{:S(2)}) collective-permute-start(bf16[32,128,128]{2,1,0:T(8,128)(2,1)S(1)} %all-to-all-done.1.own), channel_id=1, source_target_pairs={{0,1},{1,0},{2,3},{3,2},{4,5},{5,4},{6,7},{7,6},{8,9},{9,8},{10,11... | collective-permute-start | bytes 3145736 | tf_op jit(solution)/shard_map/ppermute | solution.py:275
  117.1 1.7 copy-start.3
  154.9 18.6 %all-to-all-start.3 = ((bf16[8,192,128]{2,1,0:T(8,128)(2,1)}), bf16[8,192,128]{2,1,0:T(8,128)(2,1)S(1)}, u32[]{:S(2)}, u32[]{:S(2)}) async-start(bf16[8,192,128]{2,1,0:T(8,128)(2,1)} %bitcast.9), calls=%async_computation.4 | async-start | bytes 786432 | tf_op jit(solution)/shard_map/all_to_all | solution.py:311
Sparse Core Ops, SparseCore 0:
  67.1 35.1 all-gather.3
  154.2 40.6 reduce-scatter.1
